TPU v7x, 512 devices: a whole 4x8x8 slice. The times are simulated.
512 devices in a mesh: ta: 16 (over x_lo, z), ha: 32 (over y, x_hi, core).
Axes of the slice: x: 4 (x_hi: 2, x_lo: 2; x = x_hi * 2 + x_lo), y: 8, z: 8, core: 2. Of those that a mesh axis runs over, the one named last changes fastest.
Arguments:
- queries: bfloat16 [16, 512, 8, 2048], P('ta', 'ha'), may hold values from -6 to 6
- keys: bfloat16 [16, 512, 8, 2048], P('ta', 'ha'), may hold values from -6 to 6
- values: bfloat16 [16, 512, 8, 2048], P('ta', 'ha'), may hold values from -6 to 6
- out_grad: bfloat16 [16, 512, 8, 2048], P('ta', 'ha'), may hold values from -96 to 96
- log_sum_exp: float32 [16, 16, 4096], P(None, 'ta', 'ha'), may hold values from 7.3 to 8.5
- row_delta: float32 [16, 16, 4096], P(None, 'ta', 'ha'), may hold values from -600 to 600
- time_start: int32 [16, 4], replicated, may hold values from 0 to 1, as said below
- height_start: int32 [16, 64], replicated, may hold values from 0 to 61, as said below
- head_order: int32 [16], replicated, may hold values from 0 to 15, each once
Outputs:
- query_grad: bfloat16 [16, 512, 8, 2048], P('ta', 'ha')
- key_grad: bfloat16 [16, 512, 8, 2048], P('ta', 'ha')
- value_grad: bfloat16 [16, 512, 8, 2048], P('ta', 'ha')
Inputs may be any that keep to these rules, and one draw needn't show every extreme that they name: time_start[m, a] lies between a - 2 and a, so the window holds tile a. height_start[m, c] lies between c - 2 and c, so the window holds tile c. `head_order`: each model head appears in exactly one slot.
All inputs are finite; a program needn't handle non-finite values.
Results may differ from a plain program's by a relative error of at most 0.0054.
Values may be sent and summed in bfloat16 or wider, within the bound.
A program may use at most 64 MiB of HBM per device.

v0:
```python
import jax
import jax.numpy as jnp
from jax import lax
from jax.sharding import PartitionSpec as P

HD = 128
TILE_T = 4
TILE_H = 8


def extended(cells, sides, width):
    for axis, dim in sides:
        count = lax.axis_size(axis)
        ends = count - 1
        head = lax.slice_in_dim(cells, 0, width, axis=dim)
        tail = lax.slice_in_dim(cells, cells.shape[dim] - width, cells.shape[dim], axis=dim)
        cells = jnp.concatenate(
            [
                lax.ppermute(tail, axis, [(i, (i + 1) % count) for i in range(ends)]),
                cells,
                lax.ppermute(head, axis, [((i + 1) % count, i) for i in range(ends)]),
            ],
            axis=dim,
        )
    return cells


def block_grads(query_rows, grad_rows, lse_rows, delta_rows, key_window, value_window):
    factor = HD ** (-0.5)
    pair_dims = (((2,), (2,)), ((0,), (0,)))
    scores = (
        lax.dot_general(query_rows, key_window, pair_dims, preferred_element_type=jnp.float32)
        * factor
    )
    probs_high = jnp.exp(scores - lse_rows[:, :, None])
    probs_low = probs_high.astype(jnp.bfloat16)
    dprob_high = lax.dot_general(
        grad_rows, value_window, pair_dims, preferred_element_type=jnp.float32
    )
    dscore = probs_high * (dprob_high - delta_rows[:, :, None])
    dscore_low = dscore.astype(jnp.bfloat16)
    query_part = factor * lax.dot_general(
        dscore_low, key_window, (((2,), (1,)), ((0,), (0,))), preferred_element_type=jnp.float32
    )
    back_dims = (((1,), (1,)), ((0,), (0,)))
    key_part = factor * lax.dot_general(
        dscore_low, query_rows, back_dims, preferred_element_type=jnp.float32
    )
    value_part = lax.dot_general(
        probs_low, grad_rows, back_dims, preferred_element_type=jnp.float32
    )
    return (query_part, key_part, value_part)


def to_tiles(tensor):
    frames, height, tile_width, features = tensor.shape
    time_tiles = frames // TILE_T
    height_tiles = height // TILE_H
    head_count = features // HD
    shaped = tensor.reshape(time_tiles, TILE_T, height_tiles, TILE_H, tile_width, head_count, HD)
    shaped = shaped.transpose(5, 0, 2, 1, 3, 4, 6)
    return shaped.reshape(head_count, time_tiles, height_tiles, TILE_T * TILE_H * tile_width, HD)


def from_tiles(tiled, tile_width):
    head_count, time_tiles, height_tiles, tile_size, head_depth = tiled.shape
    shaped = tiled.reshape(
        head_count, time_tiles, height_tiles, TILE_T, TILE_H, tile_width, head_depth
    )
    shaped = shaped.transpose(1, 3, 2, 4, 5, 0, 6)
    return shaped.reshape(
        time_tiles * TILE_T, height_tiles * TILE_H, tile_width, head_count * head_depth
    )


def stat_tiles(stat_rows, tile_width):
    head_count, frames, cells = stat_rows.shape
    time_tiles = frames // TILE_T
    height_tiles = cells // (TILE_H * tile_width)
    shaped = stat_rows.reshape(head_count, time_tiles, TILE_T, height_tiles, TILE_H * tile_width)
    shaped = shaped.transpose(0, 1, 3, 2, 4)
    return shaped.reshape(head_count, time_tiles, height_tiles, TILE_T * TILE_H * tile_width)


def per_device(
    queries, keys, values, out_grad, log_sum_exp, row_delta, time_start, height_start, head_order
):
    row_count = queries.shape[1]
    tile_width = queries.shape[2]
    head_query, head_keys, head_values, head_grad = (
        lax.all_to_all(queries, "ta", split_axis=3, concat_axis=0, tiled=True),
        lax.all_to_all(keys, "ta", split_axis=3, concat_axis=0, tiled=True),
        lax.all_to_all(values, "ta", split_axis=3, concat_axis=0, tiled=True),
        lax.all_to_all(out_grad, "ta", split_axis=3, concat_axis=0, tiled=True),
    )
    window_pair = extended(jnp.stack([head_keys, head_values]), (("ha", 2),), row_count)
    head_lse, head_delta = (
        lax.all_to_all(log_sum_exp, "ta", split_axis=0, concat_axis=1, tiled=True),
        lax.all_to_all(row_delta, "ta", split_axis=0, concat_axis=1, tiled=True),
    )
    dev_tiles = row_count // TILE_H
    local_heads = head_query.shape[3] // HD
    query_tiles = to_tiles(head_query)
    grad_tiles = to_tiles(head_grad)
    window_keys = to_tiles(window_pair[0])
    window_values = to_tiles(window_pair[1])
    lse_tiles = stat_tiles(head_lse, tile_width)
    delta_tiles = stat_tiles(head_delta, tile_width)
    time_tiles = query_tiles.shape[1]
    tile_size = query_tiles.shape[3]
    slot_ids = lax.axis_index("ta") * local_heads + jnp.arange(local_heads, dtype=jnp.int32)
    all_heads = jnp.arange(head_order.shape[0], dtype=jnp.int32)
    model_heads = jnp.sum(
        jnp.where(all_heads[None, :] == slot_ids[:, None], head_order[None, :], 0), axis=1
    )
    chosen = all_heads[None, :] == model_heads[:, None]
    time_rows = jnp.sum(jnp.where(chosen[:, :, None], time_start[None], 0), axis=1)
    height_rows = jnp.sum(jnp.where(chosen[:, :, None], height_start[None], 0), axis=1)
    first_tile = dev_tiles * lax.axis_index("ha")
    height_local = (
        lax.dynamic_slice_in_dim(height_rows, first_tile, dev_tiles, 1) - first_tile + dev_tiles
    )
    zero_grads = jnp.zeros((local_heads, time_tiles, 3 * dev_tiles, tile_size, HD), jnp.float32)
    zero_query = jnp.zeros((local_heads, time_tiles, dev_tiles, tile_size, HD), jnp.bfloat16)

    def visit_tile(position, running):
        key_sums, value_sums, query_out = running
        head_slot = position // time_tiles
        time_tile = position % time_tiles
        time_first = time_rows[head_slot, time_tile]
        query_rows = query_tiles[head_slot, time_tile]
        grad_rows = grad_tiles[head_slot, time_tile]
        lse_rows = lse_tiles[head_slot, time_tile]
        delta_rows = delta_tiles[head_slot, time_tile]
        anchors = []
        key_list = []
        value_list = []
        for height_tile in range(dev_tiles):
            anchor = (
                head_slot,
                time_first,
                height_local[head_slot, height_tile],
                jnp.int32(0),
                jnp.int32(0),
            )
            anchors.append(anchor)
            key_list.append(
                lax.dynamic_slice(window_keys, anchor, (1, 3, 3, tile_size, HD)).reshape(
                    9 * tile_size, HD
                )
            )
            value_list.append(
                lax.dynamic_slice(window_values, anchor, (1, 3, 3, tile_size, HD)).reshape(
                    9 * tile_size, HD
                )
            )
        query_part, key_part, value_part = block_grads(
            query_rows, grad_rows, lse_rows, delta_rows, jnp.stack(key_list), jnp.stack(value_list)
        )
        query_new = query_part.astype(jnp.bfloat16)[None, None]
        query_out = lax.dynamic_update_slice(query_out, query_new, (head_slot, time_tile, 0, 0, 0))
        for height_tile in range(dev_tiles):
            anchor = anchors[height_tile]
            key_old = lax.dynamic_slice(key_sums, anchor, (1, 3, 3, tile_size, HD))
            key_add = key_part[height_tile].reshape(1, 3, 3, tile_size, HD)
            key_sums = lax.dynamic_update_slice(key_sums, key_old + key_add, anchor)
            value_old = lax.dynamic_slice(value_sums, anchor, (1, 3, 3, tile_size, HD))
            value_add = value_part[height_tile].reshape(1, 3, 3, tile_size, HD)
            value_sums = lax.dynamic_update_slice(value_sums, value_old + value_add, anchor)
        return (key_sums, value_sums, query_out)

    key_sums, value_sums, query_out = lax.fori_loop(
        0, local_heads * time_tiles, visit_tile, (zero_grads, zero_grads, zero_query)
    )
    gradients = jnp.stack([key_sums, value_sums])
    outgoing = jnp.concatenate(
        [gradients[:, :, :, :dev_tiles], gradients[:, :, :, 2 * dev_tiles :]], axis=3
    )
    arrived = extended(outgoing, (("ha", 3),), dev_tiles)
    summed = (
        gradients[:, :, :, dev_tiles : 2 * dev_tiles]
        + arrived[:, :, :, :dev_tiles]
        + arrived[:, :, :, 3 * dev_tiles :]
    )
    summed_low = summed.astype(jnp.bfloat16)
    grad_query = from_tiles(query_out, tile_width)
    grad_keys = from_tiles(summed_low[0], tile_width)
    grad_values = from_tiles(summed_low[1], tile_width)
    return (
        lax.all_to_all(grad_query, "ta", split_axis=0, concat_axis=3, tiled=True),
        lax.all_to_all(grad_keys, "ta", split_axis=0, concat_axis=3, tiled=True),
        lax.all_to_all(grad_values, "ta", split_axis=0, concat_axis=3, tiled=True),
    )


def solution(mesh):
    placed = (
        P("ta", "ha", None, None),
        P("ta", "ha", None, None),
        P("ta", "ha", None, None),
        P("ta", "ha", None, None),
        P(None, "ta", "ha"),
        P(None, "ta", "ha"),
        P(),
        P(),
        P(),
    )
    return jax.shard_map(
        per_device,
        mesh=mesh,
        in_specs=placed,
        out_specs=(P("ta", "ha", None, None), P("ta", "ha", None, None), P("ta", "ha", None, None)),
        check_vma=False,
    )
```

profile of v0, /device:TPU:1, one launch (start us, length us, event | category | flops | bytes accessed | tf_op | source)
XLA Modules:
  0.0 318.6 jit_solution(8169461992654426165)
XLA Ops:
  0.6 19.1 %all_to_all.132 = f32[16,1,128]{2,1,0:T(1,128)S(1)} all-to-all(f32[16,1,128]{2,1,0:T(1,128)} %param.15), channel_id=1, replica_groups=mesh['ta'=16,'ha'=32] {'ta'}, dimensions={0} | all-to-all | bytes 16384 | tf_op jit(solution)/shard_map/all_to_all | solution.py:98
  19.8 3.5 %all-to-all-start.5 = ((f32[16,1,128]{2,1,0:T(1,128)}), f32[16,1,128]{2,1,0:T(1,128)S(1)}, u32[]{:S(2)}, u32[]{:S(2)}) async-start(f32[16,1,128]{2,1,0:T(1,128)} %param.16), calls=%async_computation.5 | async-start | bytes 16384 | tf_op jit(solution)/shard_map/all_to_all | solution.py:99
  23.2 5.5 %copy.96 = bf16[1,16,8,2048]{1,2,0,3:T(8,128)(2,1)} copy(bf16[1,16,8,2048]{3,2,1,0:T(8,128)(2,1)} %param.12) | data formatting | bytes 1048576 | tf_op args[1]
  28.8 6.5 %reshape.164 = bf16[16,2,8192]{2,1,0:T(2,128)(2,1)} reshape(bf16[2048,1,8,16]{3,2,1,0:T(8,128)(2,1)} %bitcast.170) | data formatting | bytes 1048576
  35.3 7.5 %all-to-all-start.1 = ((bf16[16,2,8192]{2,1,0:T(2,128)(2,1)}), bf16[16,2,8192]{2,1,0:T(2,128)(2,1)S(1)}, u32[]{:S(2)}, u32[]{:S(2)}) async-start(bf16[16,2,8192]{2,1,0:T(2,128)(2,1)} %reshape.164), calls=%async_computation.1 | async-start | bytes 1048576 | tf_op jit(solution)/shard_map/all_to_all | solution.py:92
  42.8 4.2 %copy.98 = bf16[1,16,8,2048]{1,2,0,3:T(8,128)(2,1)} copy(bf16[1,16,8,2048]{3,2,1,0:T(8,128)(2,1)S(1)} %copy-done.6) | data formatting | bytes 1048576 | tf_op args[2]
  47.0 6.5 %reshape.162 = bf16[16,2,8192]{2,1,0:T(2,128)(2,1)} reshape(bf16[2048,1,8,16]{3,2,1,0:T(8,128)(2,1)} %bitcast.171) | data formatting | bytes 1048576
  55.1 6.8 %all-to-all-start.2 = ((bf16[16,2,8192]{2,1,0:T(2,128)(2,1)}), bf16[16,2,8192]{2,1,0:T(2,128)(2,1)S(1)}, u32[]{:S(2)}, u32[]{:S(2)}) async-start(bf16[16,2,8192]{2,1,0:T(2,128)(2,1)} %reshape.162), calls=%async_computation.2 | async-start | bytes 1048576 | tf_op jit(solution)/shard_map/all_to_all | solution.py:93
  61.8 4.2 %copy.92 = bf16[1,16,8,2048]{1,2,0,3:T(8,128)(2,1)} copy(bf16[1,16,8,2048]{3,2,1,0:T(8,128)(2,1)S(1)} %copy-done.7) | data formatting | bytes 1048576 | tf_op args[0]
  66.1 6.4 %reshape.160 = bf16[16,2,8192]{2,1,0:T(2,128)(2,1)} reshape(bf16[2048,1,8,16]{3,2,1,0:T(8,128)(2,1)} %bitcast.172) | data formatting | bytes 1048576
  74.2 6.7 %all-to-all-start = ((bf16[16,2,8192]{2,1,0:T(2,128)(2,1)}), bf16[16,2,8192]{2,1,0:T(2,128)(2,1)S(1)}, u32[]{:S(2)}, u32[]{:S(2)}) async-start(bf16[16,2,8192]{2,1,0:T(2,128)(2,1)} %reshape.160), calls=%async_computation | async-start | bytes 1048576 | tf_op jit(solution)/shard_map/all_to_all | solution.py:91
  80.9 4.1 %reshape.165 = bf16[2048,1,8,16]{3,2,1,0:T(8,128)(2,1)} reshape(bf16[16,2,8192]{2,1,0:T(2,128)(2,1)S(1)} %all-to-all-done.1) | data formatting | bytes 1048576
  85.0 4.8 %copy.119 = bf16[1,16,8,16,128]{4,3,2,1,0:T(8,128)(2,1)S(1)} copy(bf16[1,16,8,16,128]{1,2,4,3,0:T(8,128)(2,1)} %bitcast.166) | data formatting | bytes 1048576 | tf_op jit(solution)/shard_map/all_to_all | solution.py:92
  89.8 4.1 %reshape.163 = bf16[2048,1,8,16]{3,2,1,0:T(8,128)(2,1)} reshape(bf16[16,2,8192]{2,1,0:T(2,128)(2,1)S(1)} %all-to-all-done.2) | data formatting | bytes 1048576
  93.9 4.9 %copy.120 = bf16[1,16,8,16,128]{4,3,2,1,0:T(8,128)(2,1)S(1)} copy(bf16[1,16,8,16,128]{1,2,4,3,0:T(8,128)(2,1)} %bitcast.167) | data formatting | bytes 1048576 | tf_op jit(solution)/shard_map/all_to_all | solution.py:93
  98.9 4.1 %collective-permute-start.1 = (bf16[2,16,16,8,128]{4,1,3,2,0:T(8,128)(2,1)S(1)}, bf16[2,16,16,8,128]{4,1,3,2,0:T(8,128)(2,1)}, u32[]{:S(2)}, u32[]{:S(2)}) collective-permute-start(bf16[2,16,16,8,128]{4,1,3,2,0:T(8,128)(2,1)S(1)} %pad_maximum_fusion.5), channel_id=1, source_target_pairs={{1,0},{2,1},{3,2},{4,3},{5,4},{6,5},{7,6},{8,7},{9,8},{10,9},{11,1... | collective-permute-start | bytes 3145736 | tf_op jit(solution)/shard_map/ppermute | solution.py:21
  103.0 4.4 %collective-permute-start = (bf16[2,16,16,8,128]{4,1,3,2,0:T(8,128)(2,1)S(1)}, bf16[2,16,16,8,128]{4,1,3,2,0:T(8,128)(2,1)}, u32[]{:S(2)}, u32[]{:S(2)}) collective-permute-start(bf16[2,16,16,8,128]{4,1,3,2,0:T(8,128)(2,1)S(1)} %pad_maximum_fusion.5), channel_id=1, source_target_pairs={{0,1},{1,2},{2,3},{3,4},{4,5},{5,6},{6,7},{7,8},{8,9},{9,10},{10,1... | collective-permute-start | bytes 3145736 | tf_op jit(solution)/shard_map/ppermute | solution.py:19
  107.5 4.2 %copy.103 = bf16[1,16,8,2048]{1,2,0,3:T(8,128)(2,1)} copy(bf16[1,16,8,2048]{3,2,1,0:T(8,128)(2,1)S(1)} %copy-done.8) | data formatting | bytes 1048576 | tf_op args[3]
  111.7 6.5 %reshape.166 = bf16[16,2,8192]{2,1,0:T(2,128)(2,1)} reshape(bf16[2048,1,8,16]{3,2,1,0:T(8,128)(2,1)} %bitcast.173) | data formatting | bytes 1048576
  118.2 7.2 %all-to-all-start.4 = ((bf16[16,2,8192]{2,1,0:T(2,128)(2,1)}), bf16[16,2,8192]{2,1,0:T(2,128)(2,1)S(1)}, u32[]{:S(2)}, u32[]{:S(2)}) async-start(bf16[16,2,8192]{2,1,0:T(2,128)(2,1)} %reshape.166), calls=%async_computation.4 | async-start | bytes 1048576 | tf_op jit(solution)/shard_map/all_to_all | solution.py:94
  133.7 4.1 %reshape.161 = bf16[2048,1,8,16]{3,2,1,0:T(8,128)(2,1)} reshape(bf16[16,2,8192]{2,1,0:T(2,128)(2,1)S(1)} %all-to-all-done) | data formatting | bytes 1048576
  137.8 4.8 %copy.118 = bf16[1,16,8,16,128]{4,3,2,1,0:T(8,128)(2,1)S(1)} copy(bf16[1,16,8,16,128]{1,2,4,3,0:T(8,128)(2,1)} %bitcast.168) | data formatting | bytes 1048576 | tf_op jit(solution)/shard_map/all_to_all | solution.py:91
  143.6 4.1 %reshape.167 = bf16[2048,1,8,16]{3,2,1,0:T(8,128)(2,1)} reshape(bf16[16,2,8192]{2,1,0:T(2,128)(2,1)S(1)} %all-to-all-done.4) | data formatting | bytes 1048576
  147.7 4.8 %copy.121 = bf16[1,16,8,16,128]{4,3,2,1,0:T(8,128)(2,1)S(1)} copy(bf16[1,16,8,16,128]{1,2,4,3,0:T(8,128)(2,1)} %bitcast.169) | data formatting | bytes 1048576 | tf_op jit(solution)/shard_map/all_to_all | solution.py:94
  163.0 56.9 %while.19 = (s32[]{:T(128)}, f32[1,4,6,256,128]{4,3,2,1,0:T(8,128)}, f32[1,4,6,256,128]{4,3,2,1,0:T(8,128)S(1)}, bf16[1,4,2,256,128]{4,3,2,1,0:T(8,128)(2,1)}, s...) while((s32[]{:T(128)}, ...), condition=%wide.region_4.5_spmd, body=%wide.region_3.4_spmd.sunk | while | flops 1520697344 | bytes 94122496 | solution.py:172
  219.9 4.0 %fusion.29 = (f32[2,1,4,2,256,128]{5,4,3,2,1,0:T(8,128)}, f32[2,1,4,2,256,128]{5,4,3,2,1,0:T(8,128)}) fusion(f32[1,1,4,6,256,128]{5,4,3,2,1,0:T(8,128)} %bitcast.152, f32[1,1,4,6,256,128]{5,4,3,2,1,0:T(8,128)S(1)} %bitcast.150), kind=kLoop, calls=%fused_computation.50 | loop fusion | flops 1048576 | bytes 10485760 | tf_op jit(solution)/shard_map/stack | solution.py:175
  230.4 7.6 %all-to-all-start.6 = ((bf16[16,16,8,128]{3,2,1,0:T(8,128)(2,1)}), bf16[16,16,8,128]{3,2,1,0:T(8,128)(2,1)}, u32[]{:S(2)}, u32[]{:S(2)}) async-start(bf16[16,16,8,128]{3,2,1,0:T(8,128)(2,1)} %bitcast.184), calls=%async_computation.6 | async-start | bytes 1048576 | tf_op jit(solution)/shard_map/all_to_all | solution.py:190
  238.0 43.0 %collective-permute-done.2 = f32[2,1,4,2,256,128]{5,4,3,2,1,0:T(8,128)} collective-permute-done((f32[2,1,4,2,256,128]{5,4,3,2,1,0:T(8,128)}, f32[2,1,4,2,256,128]{5,4,3,2,1,0:T(8,128)}, u32[]{:S(2)}, u32[]{:S(2)}) %collective-permute-start.2) | collective-permute-done | bytes 2097184 | tf_op jit(solution)/shard_map/ppermute | solution.py:19
  284.8 7.2 %all-to-all-start.7 = ((bf16[16,16,8,128]{3,2,1,0:T(8,128)(2,1)}), bf16[16,16,8,128]{3,2,1,0:T(8,128)(2,1)S(1)}, u32[]{:S(2)}, u32[]{:S(2)}) async-start(bf16[16,16,8,128]{3,2,1,0:T(8,128)(2,1)} %bitcast.51), calls=%async_computation.7 | async-start | bytes 1048576 | tf_op jit(solution)/shard_map/all_to_all | solution.py:191
  292.9 10.1 %all-to-all-done.7 = bf16[16,16,8,128]{3,2,1,0:T(8,128)(2,1)S(1)} async-done(((bf16[16,16,8,128]{3,2,1,0:T(8,128)(2,1)}), bf16[16,16,8,128]{3,2,1,0:T(8,128)(2,1)S(1)}, u32[]{:S(2)}, u32[]{:S(2)}) %all-to-all-start.7) | async-done | bytes 524320 | tf_op jit(solution)/shard_map/all_to_all | solution.py:191
  303.0 4.5 %all-to-all-start.8 = ((bf16[16,16,8,128]{3,2,1,0:T(8,128)(2,1)}), bf16[16,16,8,128]{3,2,1,0:T(8,128)(2,1)S(1)}, u32[]{:S(2)}, u32[]{:S(2)}) async-start(bf16[16,16,8,128]{3,2,1,0:T(8,128)(2,1)} %bitcast.56), calls=%async_computation.8 | async-start | bytes 1048576 | tf_op jit(solution)/shard_map/all_to_all | solution.py:192
  310.3 7.5 %all-to-all-done.8 = bf16[16,16,8,128]{3,2,1,0:T(8,128)(2,1)S(1)} async-done(((bf16[16,16,8,128]{3,2,1,0:T(8,128)(2,1)}), bf16[16,16,8,128]{3,2,1,0:T(8,128)(2,1)S(1)}, u32[]{:S(2)}, u32[]{:S(2)}) %all-to-all-start.8) | async-done | bytes 524320 | tf_op jit(solution)/shard_map/all_to_all | solution.py:192
  (162 shorter events, 82.8 us)
Async XLA Ops:
  19.8 15.5 %all-to-all-start.5 = ((f32[16,1,128]{2,1,0:T(1,128)}), f32[16,1,128]{2,1,0:T(1,128)S(1)}, u32[]{:S(2)}, u32[]{:S(2)}) async-start(f32[16,1,128]{2,1,0:T(1,128)} %param.16), calls=%async_computation.5 | async-start | bytes 16384 | tf_op jit(solution)/shard_map/all_to_all | solution.py:99
  28.8 14.0 %copy-start.6 = (bf16[1,16,8,2048]{3,2,1,0:T(8,128)(2,1)S(1)}, bf16[1,16,8,2048]{3,2,1,0:T(8,128)(2,1)}, u32[]{:S(2)}) copy-start(bf16[1,16,8,2048]{3,2,1,0:T(8,128)(2,1)} %param.13) | copy-start | bytes 1572868
  35.3 19.8 %all-to-all-start.1 = ((bf16[16,2,8192]{2,1,0:T(2,128)(2,1)}), bf16[16,2,8192]{2,1,0:T(2,128)(2,1)S(1)}, u32[]{:S(2)}, u32[]{:S(2)}) async-start(bf16[16,2,8192]{2,1,0:T(2,128)(2,1)} %reshape.164), calls=%async_computation.1 | async-start | bytes 1048576 | tf_op jit(solution)/shard_map/all_to_all | solution.py:92
  47.0 14.8 %copy-start.7 = (bf16[1,16,8,2048]{3,2,1,0:T(8,128)(2,1)S(1)}, bf16[1,16,8,2048]{3,2,1,0:T(8,128)(2,1)}, u32[]{:S(2)}) copy-start(bf16[1,16,8,2048]{3,2,1,0:T(8,128)(2,1)} %param.11) | copy-start | bytes 1572868
  55.1 19.1 %all-to-all-start.2 = ((bf16[16,2,8192]{2,1,0:T(2,128)(2,1)}), bf16[16,2,8192]{2,1,0:T(2,128)(2,1)S(1)}, u32[]{:S(2)}, u32[]{:S(2)}) async-start(bf16[16,2,8192]{2,1,0:T(2,128)(2,1)} %reshape.162), calls=%async_computation.2 | async-start | bytes 1048576 | tf_op jit(solution)/shard_map/all_to_all | solution.py:93
  74.2 44.0 %all-to-all-start = ((bf16[16,2,8192]{2,1,0:T(2,128)(2,1)}), bf16[16,2,8192]{2,1,0:T(2,128)(2,1)S(1)}, u32[]{:S(2)}, u32[]{:S(2)}) async-start(bf16[16,2,8192]{2,1,0:T(2,128)(2,1)} %reshape.160), calls=%async_computation | async-start | bytes 1048576 | tf_op jit(solution)/shard_map/all_to_all | solution.py:91
  93.9 13.5 %copy-start.8 = (bf16[1,16,8,2048]{3,2,1,0:T(8,128)(2,1)S(1)}, bf16[1,16,8,2048]{3,2,1,0:T(8,128)(2,1)}, u32[]{:S(2)}) copy-start(bf16[1,16,8,2048]{3,2,1,0:T(8,128)(2,1)} %param.14) | copy-start | bytes 1572868
  98.9 54.6 %collective-permute-start.1 = (bf16[2,16,16,8,128]{4,1,3,2,0:T(8,128)(2,1)S(1)}, bf16[2,16,16,8,128]{4,1,3,2,0:T(8,128)(2,1)}, u32[]{:S(2)}, u32[]{:S(2)}) collective-permute-start(bf16[2,16,16,8,128]{4,1,3,2,0:T(8,128)(2,1)S(1)} %pad_maximum_fusion.5), channel_id=1, source_target_pairs={{1,0},{2,1},{3,2},{4,3},{5,4},{6,5},{7,6},{8,7},{9,8},{10,9},{11,1... | collective-permute-start | bytes 3145736 | tf_op jit(solution)/shard_map/ppermute | solution.py:21
  103.0 50.5 %collective-permute-start = (bf16[2,16,16,8,128]{4,1,3,2,0:T(8,128)(2,1)S(1)}, bf16[2,16,16,8,128]{4,1,3,2,0:T(8,128)(2,1)}, u32[]{:S(2)}, u32[]{:S(2)}) collective-permute-start(bf16[2,16,16,8,128]{4,1,3,2,0:T(8,128)(2,1)S(1)} %pad_maximum_fusion.5), channel_id=1, source_target_pairs={{0,1},{1,2},{2,3},{3,4},{4,5},{5,6},{6,7},{7,8},{8,9},{9,10},{10,1... | collective-permute-start | bytes 3145736 | tf_op jit(solution)/shard_map/ppermute | solution.py:19
  111.7 13.7 %copy-start.11 = (s32[16]{0:T(128)S(1)}, s32[16]{0:T(128)}, u32[]{:S(2)}) copy-start(s32[16]{0:T(128)} %param.19) | copy-start | bytes 196
  111.7 15.0 %copy-start.9 = (s32[16,64]{1,0:T(8,128)S(1)}, s32[16,64]{1,0:T(8,128)}, u32[]{:S(2)}) copy-start(s32[16,64]{1,0:T(8,128)} %param.18) | copy-start | bytes 12292
  111.7 19.7 %copy-start.10 = (s32[16,4]{0,1:T(4,128)S(1)}, s32[16,4]{0,1:T(4,128)}, u32[]{:S(2)}) copy-start(s32[16,4]{0,1:T(4,128)} %param.17) | copy-start | bytes 772
  118.2 25.4 %all-to-all-start.4 = ((bf16[16,2,8192]{2,1,0:T(2,128)(2,1)}), bf16[16,2,8192]{2,1,0:T(2,128)(2,1)S(1)}, u32[]{:S(2)}, u32[]{:S(2)}) async-start(bf16[16,2,8192]{2,1,0:T(2,128)(2,1)} %reshape.166), calls=%async_computation.4 | async-start | bytes 1048576 | tf_op jit(solution)/shard_map/all_to_all | solution.py:94
  165.5 1.8 copy-start.2
  165.5 1.8 copy-start.4
  173.0 1.9 copy-start
  175.6 1.6 copy-start.1
  179.7 1.8 copy-start.2
  179.7 1.8 copy-start.4
  187.2 1.9 copy-start
  193.9 1.8 copy-start.2
  194.0 1.8 copy-start.4
  201.4 1.9 copy-start
  208.1 1.8 copy-start.2
  208.2 1.8 copy-start.4
  215.7 1.9 copy-start
  219.9 9.6 %copy-start.5 = (bf16[1,4,2,256,128]{4,3,2,1,0:T(8,128)(2,1)S(1)}, bf16[1,4,2,256,128]{4,3,2,1,0:T(8,128)(2,1)}, u32[]{:S(2)}) copy-start(bf16[1,4,2,256,128]{4,3,2,1,0:T(8,128)(2,1)} %get-tuple-element.303) | copy-start | bytes 1572868
  223.9 57.1 %collective-permute-start.2 = (f32[2,1,4,2,256,128]{5,4,3,2,1,0:T(8,128)}, f32[2,1,4,2,256,128]{5,4,3,2,1,0:T(8,128)}, u32[]{:S(2)}, u32[]{:S(2)}) collective-permute-start(f32[2,1,4,2,256,128]{5,4,3,2,1,0:T(8,128)} %get-tuple-element.342), channel_id=1, source_target_pairs={{0,1},{1,2},{2,3},{3,4},{4,5},{5,6},{6,7},{7,8},{8,9},{9,10},{10,1... | collective-permute-start | bytes 6291464 | tf_op jit(solution)/shard_map/ppermute | solution.py:19
  227.2 53.8 %collective-permute-start.3 = (f32[2,1,4,2,256,128]{5,4,3,2,1,0:T(8,128)}, f32[2,1,4,2,256,128]{5,4,3,2,1,0:T(8,128)}, u32[]{:S(2)}, u32[]{:S(2)}) collective-permute-start(f32[2,1,4,2,256,128]{5,4,3,2,1,0:T(8,128)} %get-tuple-element.343), channel_id=1, source_target_pairs={{1,0},{2,1},{3,2},{4,3},{5,4},{6,5},{7,6},{8,7},{9,8},{10,9},{11,1... | collective-permute-start | bytes 6291464 | tf_op jit(solution)/shard_map/ppermute | solution.py:21
  230.4 54.4 %all-to-all-start.6 = ((bf16[16,16,8,128]{3,2,1,0:T(8,128)(2,1)}), bf16[16,16,8,128]{3,2,1,0:T(8,128)(2,1)}, u32[]{:S(2)}, u32[]{:S(2)}) async-start(bf16[16,16,8,128]{3,2,1,0:T(8,128)(2,1)} %bitcast.184), calls=%async_computation.6 | async-start | bytes 1048576 | tf_op jit(solution)/shard_map/all_to_all | solution.py:190
  284.8 18.2 %all-to-all-start.7 = ((bf16[16,16,8,128]{3,2,1,0:T(8,128)(2,1)}), bf16[16,16,8,128]{3,2,1,0:T(8,128)(2,1)S(1)}, u32[]{:S(2)}, u32[]{:S(2)}) async-start(bf16[16,16,8,128]{3,2,1,0:T(8,128)(2,1)} %bitcast.51), calls=%async_computation.7 | async-start | bytes 1048576 | tf_op jit(solution)/shard_map/all_to_all | solution.py:191
  303.0 14.8 %all-to-all-start.8 = ((bf16[16,16,8,128]{3,2,1,0:T(8,128)(2,1)}), bf16[16,16,8,128]{3,2,1,0:T(8,128)(2,1)S(1)}, u32[]{:S(2)}, u32[]{:S(2)}) async-start(bf16[16,16,8,128]{3,2,1,0:T(8,128)(2,1)} %bitcast.56), calls=%async_computation.8 | async-start | bytes 1048576 | tf_op jit(solution)/shard_map/all_to_all | solution.py:192
  (7 other events, 9.1 us)
where the time goes:
time: 324 us; the launch traced here: 319 us
  local copies, waits for them, and re-layouts  121 us (37%)
  starting transfers between devices  65.1 us (20%)
  waiting for transfers between devices  63.9 us (20%)
  matrix products  20.8 us (6%)
  blocking collectives  19.1 us (6%)
  other arithmetic  15.3 us (5%)
  loops' own time  8.02 us (2%)
  between operations  4.83 us (1%)
    unnamed x26, local copies, waits for them, and re-layouts  60.4 us
    ppermute x2, waiting for transfers between devices, extended(): lax.ppermute(tail, axis, [(i, (i + 1) % count) for i in range(ends)])  43 us
    all_to_all x1, blocking collectives, per_device(): lax.all_to_all(log_sum_exp, 'ta', split_axis=0, concat_axis=1, tiled=True)  19.1 us
    while x40, local copies, waits for them, and re-layouts  14.3 us
    all_to_all x1, waiting for transfers between devices, per_device(): lax.all_to_all(grad_keys, 'ta', split_axis=0, concat_axis=3, tiled=True)  10.1 us
    another operation x1, loops' own time, per_device(): lax.fori_loop(0, local_heads * time_tiles, visit_tile, (zero_grads, zero_...  8.02 us
    ppermute x2, starting transfers between devices, extended(): lax.ppermute(tail, axis, [(i, (i + 1) % count) for i in range(ends)])  7.72 us
    all_to_all x1, starting transfers between devices, per_device(): lax.all_to_all(grad_query, 'ta', split_axis=0, concat_axis=3, tiled=True)  7.6 us
  transfers between devices with their start and end apart: 12, of which 5 were waited for; matrix products, arithmetic and copies ran while one was open for 30% of the time, Pallas kernels for 0%

commit v1 on v0

v1 whole, which is shorter than its diff:
```python
import functools

import jax
import jax.numpy as jnp
from jax import lax
from jax.experimental import pallas as pl
from jax.experimental.pallas import tpu as pltpu
from jax.sharding import PartitionSpec as P

HD = 128
SCALE = HD ** -0.5
LOG2E = 1.4426950408889634
NT = 16
NH = 32
TOK = 128
HALF = 64
SPAN = 3 * HALF
MESH = pl.DeviceIdType.MESH


def dot(a, b, dims):
    return lax.dot_general(a, b, (dims, ((), ())), preferred_element_type=jnp.float32)


def grads_kernel(
    order, time_start, height_start, lse, delta, queries, keys, values, out_grad,
    query_out, key_out, value_out,
    key_buf, value_buf, query_buf, grad_buf, lse_buf, delta_buf,
    key_window, value_window, key_parts, value_parts, key_sum, value_sum,
    query_low, key_low, value_low,
    key_send, value_send, key_recv, value_recv,
    stat_ss, stat_rs, kv_ss, kv_rs, qg_ss, qg_rs, own_sem,
    halo_ss, halo_rs, back_ss, back_rs, qo_ss, qo_rs, kvo_ss, kvo_rs,
):
    ta = lax.axis_index("ta")
    ha = lax.axis_index("ha")
    core = lax.rem(ha, 2)
    x_hi = lax.rem(ha // 2, 2)
    head = lax.rem(ta + 8 * x_hi, NT)

    def peer(d):
        return lax.rem(ta + d, NT)

    def head_of(p):
        return lax.rem(p + 8 * x_hi, NT)

    def columns(h):
        return pl.ds(pl.multiple_of(h * HD, HD), HD)

    left = (lax.rem(ta + 8 * (1 - core), NT), lax.rem(ha + NH - 1, NH))
    right = (lax.rem(ta + 8 * core, NT), lax.rem(ha + 1, NH))
    sides = (left, right)

    barrier = pltpu.get_barrier_semaphore()

    @pl.loop(1, NT)
    def _(d):
        pl.semaphore_signal(barrier, inc=1, device_id=(peer(d), ha), device_id_type=MESH)

    for side in sides:
        pl.semaphore_signal(barrier, inc=1, device_id=side, device_id_type=MESH)
    pl.semaphore_wait(barrier, NT + 1)

    def remote(src, dst, send_sem, recv_sem, device):
        return pltpu.make_async_remote_copy(
            src_ref=src, dst_ref=dst, send_sem=send_sem, recv_sem=recv_sem,
            device_id=device, device_id_type=MESH,
        )

    def stat_copy(n, d):
        p = peer(d)
        src, dst = ((lse, lse_buf), (delta, delta_buf))[n]
        return remote(src.at[head_of(p)], dst.at[ta], stat_ss.at[n, d], stat_rs.at[n, d], (p, ha))

    def kv_copy(n, d):
        p = peer(d)
        src, dst = ((keys, key_buf), (values, value_buf))[n]
        return remote(
            src.at[:, columns(head_of(p))], dst.at[ta, pl.ds(TOK, TOK), :],
            kv_ss.at[n, d], kv_rs.at[n, d], (p, ha),
        )

    def qg_copy(n, c, d):
        p = peer(d)
        src, dst = ((queries, query_buf), (out_grad, grad_buf))[n]
        return remote(
            src.at[pl.ds(c * HALF, HALF), columns(head_of(p))], dst.at[c, ta],
            qg_ss.at[n, c, d], qg_rs.at[n, c, d], (p, ha),
        )

    own = [
        pltpu.make_async_copy(keys.at[:, columns(head)], key_buf.at[ta, pl.ds(TOK, TOK), :], own_sem.at[0]),
        pltpu.make_async_copy(values.at[:, columns(head)], value_buf.at[ta, pl.ds(TOK, TOK), :], own_sem.at[1]),
        pltpu.make_async_copy(lse.at[head], lse_buf.at[ta], own_sem.at[2]),
        pltpu.make_async_copy(delta.at[head], delta_buf.at[ta], own_sem.at[3]),
    ]
    for c in range(2):
        for n, (src, dst) in enumerate(((queries, query_buf), (out_grad, grad_buf))):
            own.append(
                pltpu.make_async_copy(
                    src.at[pl.ds(c * HALF, HALF), columns(head)], dst.at[c, ta], own_sem.at[4 + 2 * c + n]
                )
            )

    for n in range(2):
        @pl.loop(1, NT)
        def _(d, n=n):
            kv_copy(n, d).start()
    for n in range(2):
        @pl.loop(1, NT)
        def _(d, n=n):
            stat_copy(n, d).start()
    for c in range(2):
        for n in range(2):
            @pl.loop(1, NT)
            def _(d, n=n, c=c):
                qg_copy(n, c, d).start()
    for copy in own:
        copy.start()

    for copy in own:
        copy.wait()

    halos = []
    for n, buf in enumerate((key_buf, value_buf)):
        @pl.loop(1, NT)
        def _(d, n=n):
            kv_copy(n, d).wait_recv()

        for s in range(2):
            copy = remote(
                buf.at[:, pl.ds(TOK, TOK), :],
                buf.at[:, pl.ds(2 * TOK * (1 - s), TOK), :],
                halo_ss.at[n, s], halo_rs.at[n, s], sides[s],
            )
            copy.start()
            halos.append(copy)

    for n in range(2):
        @pl.loop(1, NT)
        def _(d, n=n):
            stat_copy(n, d).wait_recv()
    for copy in halos:
        copy.wait_recv()

    model_head = order[head]

    def pick(table, column):
        entry = table[0, column]
        for m in range(1, NT):
            entry = jnp.where(model_head == m, table[m, column], entry)
        return entry

    early = [None] + [pick(time_start, a) == 0 for a in (1, 2)]
    low_lane = lax.broadcasted_iota(jnp.int32, (1, HD), 1) < HALF

    def stat_row(buf, a, c):
        rows = [buf[4 * a + i] for i in range(4)]
        flipped = [pltpu.roll(row, HALF, 1) for row in rows]
        if c == 0:
            pairs = [jnp.where(low_lane, rows[2 * i], flipped[2 * i + 1]) for i in range(2)]
        else:
            pairs = [jnp.where(low_lane, flipped[2 * i], rows[2 * i + 1]) for i in range(2)]
        return jnp.concatenate(pairs, axis=1)

    def query_copy(c, frame):
        return remote(
            query_low.at[c, frame], query_out.at[pl.ds(c * HALF, HALF), columns(head)],
            qo_ss.at[c, frame], qo_rs.at[c, ta], (frame, ha),
        )

    def query_own(c):
        return pltpu.make_async_copy(
            query_low.at[c, ta], query_out.at[pl.ds(c * HALF, HALF), columns(head)], qo_ss.at[c, ta]
        )

    for c in range(2):
        for n in range(2):
            @pl.loop(1, NT)
            def _(d, n=n, c=c):
                qg_copy(n, c, d).wait_recv()

        step = pick(height_start, 2 * ha + c) - (2 * ha + c) + 2
        at = [step == d for d in range(3)]

        @pl.loop(0, NT)
        def _(frame, c=c, at=at):
            for buf, window in ((key_buf, key_window), (value_buf, value_window)):
                spans = [buf[frame, pl.ds(HALF * (c + d), SPAN), :] for d in range(3)]
                window[frame] = jnp.where(at[0], spans[0], jnp.where(at[1], spans[1], spans[2]))

        @pl.loop(0, 4)
        def _(a, c=c):
            soon = pick(time_start, a) == 0

            def tile(window, j):
                now = window[pl.ds(4 * j, 4)]
                later = window[pl.ds(4 * j + 4, 4)]
                return jnp.where(soon, now, later).reshape(4 * SPAN, HD)

            query = query_buf[c, pl.ds(4 * a, 4)].reshape(4 * HALF, HD)
            grad = grad_buf[c, pl.ds(4 * a, 4)].reshape(4 * HALF, HD)
            lse_row = stat_row(lse_buf, a, c) * LOG2E
            delta_row = stat_row(delta_buf, a, c)
            turned = jnp.zeros((HD, 4 * HALF), jnp.float32)
            for j in range(3):
                key = tile(key_window, j)
                value = tile(value_window, j)
                scores = dot(key, query, ((1,), (1,)))
                probs = jnp.exp2(scores * (SCALE * LOG2E) - lse_row)
                dprob = dot(value, grad, ((1,), (1,)))
                dscore = (probs * (dprob - delta_row)).astype(jnp.bfloat16)
                value_parts[3 * a + j] = dot(
                    probs.astype(jnp.bfloat16), grad, ((1,), (0,))
                ).reshape(4, SPAN, HD)
                key_parts[3 * a + j] = dot(dscore, query, ((1,), (0,))).reshape(4, SPAN, HD)
                turned = turned + dot(key, dscore, ((0,), (0,)))
            query_low[c, pl.ds(4 * a, 4)] = (
                (turned.T * SCALE).astype(jnp.bfloat16).reshape(4, HALF, HD)
            )
            for i in range(4):
                frame = 4 * a + i

                @pl.when(frame != ta)
                def _(frame=frame):
                    query_copy(c, frame).start()

                @pl.when(frame == ta)
                def _():
                    query_own(c).start()

        back = []
        for n, (parts, total, send) in enumerate(
            ((key_parts, key_sum, key_send), (value_parts, value_sum, value_send))
        ):
            for t in range(4):
                @pl.loop(0, 4)
                def _(i, parts=parts, total=total, send=send, t=t, c=c, at=at):
                    frame = 4 * t + i
                    blank = jnp.zeros((SPAN, HD), jnp.float32)
                    found = blank
                    for a in range(4):
                        now = parts[3 * a + t, i] if t < 3 and a < 3 else blank
                        later = parts[3 * a + t - 1, i] if t > 0 and a > 0 else blank
                        if a == 0:
                            found = now
                        elif a == 3:
                            found = found + later
                        else:
                            found = found + jnp.where(early[a], now, later)
                    one, two, three = (found[HALF * e : HALF * (e + 1)] for e in range(3))
                    none = blank[:HALF]
                    placed = [
                        jnp.where(at[0], one, none),
                        jnp.where(at[0], two, jnp.where(at[1], one, none)),
                        jnp.where(at[0], three, jnp.where(at[1], two, one)),
                        jnp.where(at[1], three, jnp.where(at[2], two, none)),
                        jnp.where(at[2], three, none),
                    ]
                    if c == 0:
                        for e in range(5):
                            total[frame, HALF * e : HALF * (e + 1), :] = placed[e]
                    else:
                        low = jnp.bfloat16
                        both = [total[frame, HALF * e : HALF * (e + 1), :] + placed[e - 1] for e in range(1, 5)]
                        send[0, frame, 0:HALF, :] = total[frame, 0:HALF, :].astype(low)
                        send[0, frame, HALF:TOK, :] = both[0].astype(low)
                        total[frame, TOK : TOK + HALF, :] = both[1]
                        total[frame, TOK + HALF : 2 * TOK, :] = both[2]
                        send[1, frame, 0:HALF, :] = both[3].astype(low)
                        send[1, frame, HALF:TOK, :] = placed[4].astype(low)

            if c == 1:
                recv = (key_recv, value_recv)[n]
                for s in range(2):
                    copy = remote(
                        send.at[s], recv.at[1 - s], back_ss.at[n, s], back_rs.at[n, 1 - s], sides[s]
                    )
                    copy.start()
                    back.append(copy)

    def grad_copy(n, d):
        p = peer(d)
        low, out = ((key_low, key_out), (value_low, value_out))[n]
        return remote(
            low.at[p], out.at[:, columns(head)], kvo_ss.at[n, d], kvo_rs.at[n, d], (p, ha)
        )

    own_out = []
    for n, (total, recv, low, out) in enumerate(
        ((key_sum, key_recv, key_low, key_out), (value_sum, value_recv, value_low, value_out))
    ):
        for s in range(2):
            back[2 * n + s].wait_recv()
        factor = SCALE if n == 0 else 1.0

        @pl.loop(0, NT)
        def _(frame, total=total, recv=recv, low=low, factor=factor):
            whole = (
                total[frame, 128:256, :]
                + recv[0, frame].astype(jnp.float32)
                + recv[1, frame].astype(jnp.float32)
            )
            low[frame] = (whole * factor).astype(jnp.bfloat16)

        @pl.loop(1, NT)
        def _(d, n=n):
            grad_copy(n, d).start()

        copy = pltpu.make_async_copy(low.at[ta], out.at[:, columns(head)], own_sem.at[n])
        copy.start()
        own_out.append(copy)

    for n in range(2):
        @pl.loop(1, NT)
        def _(d, n=n):
            stat_copy(n, d).wait_send()
            kv_copy(n, d).wait_send()
            for c in range(2):
                qg_copy(n, c, d).wait_send()
    for copy in halos + back:
        copy.wait_send()
    for c in range(2):
        query_own(c).wait()

        @pl.loop(1, NT)
        def _(d, c=c):
            frame = peer(d)
            done = remote(
                query_low.at[c, frame], query_out.at[pl.ds(c * HALF, HALF), columns(head_of(frame))],
                qo_ss.at[c, frame], qo_rs.at[c, frame], (frame, ha),
            )
            done.wait_send()
            done.wait_recv()

    for n in range(2):
        @pl.loop(1, NT)
        def _(d, n=n):
            grad_copy(n, d).wait()

    for copy in own_out:
        copy.wait()


def per_device(
    queries, keys, values, out_grad, log_sum_exp, row_delta, time_start, height_start, head_order
):
    width = NT * HD
    flat = [x.reshape(TOK, width) for x in (queries, keys, values, out_grad)]
    smem = pl.BlockSpec(memory_space=pltpu.SMEM)
    hbm = pl.BlockSpec(memory_space=pl.ANY)
    bf16, f32 = jnp.bfloat16, jnp.float32
    dma = pltpu.SemaphoreType.DMA
    outs = pl.pallas_call(
        grads_kernel,
        name="tile_attention_grads",
        out_shape=[jax.ShapeDtypeStruct((TOK, width), bf16)] * 3,
        in_specs=[smem] * 3 + [hbm] * 6,
        out_specs=[hbm] * 3,
        scratch_shapes=[
            pltpu.VMEM((NT, 3 * TOK, HD), bf16),
            pltpu.VMEM((NT, 3 * TOK, HD), bf16),
            pltpu.VMEM((2, NT, HALF, HD), bf16),
            pltpu.VMEM((2, NT, HALF, HD), bf16),
            pltpu.VMEM((NT, 1, TOK), f32),
            pltpu.VMEM((NT, 1, TOK), f32),
            pltpu.VMEM((NT, SPAN, HD), bf16),
            pltpu.VMEM((NT, SPAN, HD), bf16),
            pltpu.VMEM((12, 4, SPAN, HD), f32),
            pltpu.VMEM((12, 4, SPAN, HD), f32),
            pltpu.VMEM((NT, 3 * TOK, HD), f32),
            pltpu.VMEM((NT, 3 * TOK, HD), f32),
            pltpu.VMEM((2, NT, HALF, HD), bf16),
            pltpu.VMEM((NT, TOK, HD), bf16),
            pltpu.VMEM((NT, TOK, HD), bf16),
            pltpu.VMEM((2, NT, TOK, HD), bf16),
            pltpu.VMEM((2, NT, TOK, HD), bf16),
            pltpu.VMEM((2, NT, TOK, HD), bf16),
            pltpu.VMEM((2, NT, TOK, HD), bf16),
            dma((2, NT)), dma((2, NT)),
            dma((2, NT)), dma((2, NT)),
            dma((2, 2, NT)), dma((2, 2, NT)),
            dma((8,)),
            dma((2, 2)), dma((2, 2)),
            dma((2, 2)), dma((2, 2)),
            dma((2, NT)), dma((2, NT)),
            dma((2, NT)), dma((2, NT)),
        ],
        compiler_params=pltpu.CompilerParams(
            collective_id=0, has_side_effects=True, vmem_limit_bytes=58 * 2**20
        ),
    )(head_order, time_start, height_start, log_sum_exp, row_delta, *flat)
    return tuple(x.reshape(queries.shape) for x in outs)


def solution(mesh):
    rows = P("ta", "ha", None, None)
    stats = P(None, "ta", "ha")
    return jax.shard_map(
        per_device,
        mesh=mesh,
        in_specs=(rows, rows, rows, rows, stats, stats, P(), P(), P()),
        out_specs=(rows, rows, rows),
        check_vma=False,
    )
```

time: 324 us -> 118 us (0.36); the launches traced: 319 us -> 117 us
  local copies, waits for them, and re-layouts: 121 us -> 5.32 us
  Pallas kernels: 0 us -> 111 us
  starting transfers between devices: 65.1 us -> 0 us
  waiting for transfers between devices: 63.9 us -> 0 us
  matrix products: 20.8 us -> 0 us
  blocking collectives: 19.1 us -> 0 us
  other arithmetic: 15.3 us -> 0 us
  loops' own time: 8.02 us -> 0 us
  between operations: 4.83 us -> 0.66 us
    pallas_call x0 -> x1, Pallas kernels: none -> 111 us  [per_device(): pl.pallas_call(grads_kernel, name='tile_attention_grads', out_shape=[jax....]
    unnamed x26 -> x10, local copies, waits for them, and re-layouts: 60.4 us -> 5.32 us
    all_to_all x8 -> x0, starting transfers between devices: 51 us -> none  [the longest x1 7.6 us: per_device(): lax.all_to_all(grad_query, 'ta', split_axis=0, concat_axis=3, tiled=True)]
    ppermute x4 -> x0, waiting for transfers between devices: 43 us -> none  [the longest x2 43 us: extended(): lax.ppermute(tail, axis, [(i, (i + 1) % count) for i in range(ends)])]
    all_to_all x10 -> x0, local copies, waits for them, and re-layouts: 23.8 us -> none  [the longest x2 4.97 us: per_device(): lax.all_to_all(queries, 'ta', split_axis=3, concat_axis=0, tiled=True)]
    all_to_all x8 -> x0, waiting for transfers between devices: 20.9 us -> none  [the longest x1 10.1 us: per_device(): lax.all_to_all(grad_keys, 'ta', split_axis=0, concat_axis=3, tiled=True)]
    dot_general x20 -> x0, matrix products: 20.8 us -> none  [the longest x4 5.72 us: block_grads(): lax.dot_general(dscore_low, key_window, (((2,), (1,)), ((0,), (0,))), pre...]
    all_to_all x1 -> x0, blocking collectives: 19.1 us -> none  [per_device(): lax.all_to_all(log_sum_exp, 'ta', split_axis=0, concat_axis=1, tiled=True)]
  transfers between devices with their start and end apart: 12 -> 0, of which waited for: 5 -> 0; matrix products, arithmetic and copies ran while one was open for 30% -> 0% of each run, Pallas kernels for 0% -> 0%
where the time goes in v1:
time: 118 us; the launch traced here: 117 us
  Pallas kernels  111 us (94%)
  local copies, waits for them, and re-layouts  5.32 us (5%)
    pallas_call x1, Pallas kernels, per_device(): pl.pallas_call(grads_kernel, name='tile_attention_grads', out_shape=[jax....  111 us
    unnamed x10, local copies, waits for them, and re-layouts  5.32 us

profile of v1, /device:TPU:1, one launch (start us, length us, event | category | flops | bytes accessed | tf_op | source)
XLA Modules:
  0.0 117.4 jit_solution(6856238511682454019)
XLA Ops:
  0.6 0.0 copy-start.2
  0.6 0.7 copy-done.2
  1.3 0.7 copy.12.time_start
  2.0 111.4 %tile_attention_grads.1 = (bf16[128,2048]{1,0:T(8,128)(2,1)}, bf16[128,2048]{1,0:T(8,128)(2,1)}, bf16[128,2048]{1,0:T(8,128)(2,1)}) custom-call(s32[16]{0:T(128)} %order.1, s32[16,4]{1,0:T(8,128)} %copy.12.time_start, s32[16,64]{1,0:T(8,128)} %height_start.1, f32[16,1,128]{2,1,0:T(1,128)} %lse.1, f32[16,1,128]{2,1,0:T(1,128)} %delta.1, ...), custom_call_target="tpu_custom_call" | custom-call | tf_op jit(solution)/shard_map/tile_attention_grads/pallas_call | solution.py:354
  113.4 0.0 copy-start.1
  113.4 1.9 %copy.16 = bf16[1,16,8,2048]{3,2,1,0:T(8,128)(2,1)} copy(bf16[1,16,8,2048]{3,2,1,0:T(8,128)(2,1)} %bitcast.13) | data formatting | bytes 1048576
  115.4 0.0 copy-done.1
  115.4 0.0 copy-start
  115.4 0.8 copy.17
  116.2 0.4 copy-done
  116.6 0.8 copy.18
Async XLA Ops:
  0.6 0.7 copy-start.2
  113.4 2.0 %copy-start.1 = (bf16[128,2048]{1,0:T(8,128)(2,1)S(1)}, bf16[128,2048]{1,0:T(8,128)(2,1)}, u32[]{:S(2)}) copy-start(bf16[128,2048]{1,0:T(8,128)(2,1)} %get-tuple-element.7) | copy-start | bytes 1572868
  115.4 1.2 %copy-start = (bf16[128,2048]{1,0:T(8,128)(2,1)S(1)}, bf16[128,2048]{1,0:T(8,128)(2,1)}, u32[]{:S(2)}) copy-start(bf16[128,2048]{1,0:T(8,128)(2,1)} %get-tuple-element.8) | copy-start | bytes 1572868

commit v2 on v1

v2 whole, which is shorter than its diff:
```python
import functools

import jax
import jax.numpy as jnp
from jax import lax
from jax.experimental import pallas as pl
from jax.experimental.pallas import tpu as pltpu
from jax.sharding import PartitionSpec as P

HD = 128
SCALE = HD ** -0.5
LOG2E = 1.4426950408889634
NT = 16
NH = 32
TOK = 128
HALF = 64
SPAN = 3 * HALF
MESH = pl.DeviceIdType.MESH


def dot(a, b, dims):
    return lax.dot_general(a, b, (dims, ((), ())), preferred_element_type=jnp.float32)


def grads_kernel(
    order, time_start, height_start, lse, delta, queries, keys, values, out_grad,
    query_out, key_out, value_out,
    key_buf, value_buf, query_buf, grad_buf, lse_buf, delta_buf,
    key_window, value_window, probs_buf, key_parts, value_parts,
    query_low, key_low, value_low,
    key_send, value_send, key_recv, value_recv,
    stat_ss, stat_rs, kv_ss, kv_rs, qg_ss, qg_rs, own_sem,
    halo_ss, halo_rs, back_ss, back_rs, qo_ss, qo_rs, kvo_ss, kvo_rs,
):
    ta = lax.axis_index("ta")
    ha = lax.axis_index("ha")
    core = lax.rem(ha, 2)
    x_hi = lax.rem(ha // 2, 2)
    head = lax.rem(ta + 8 * x_hi, NT)

    def peer(d):
        return lax.rem(ta + d, NT)

    def head_of(p):
        return lax.rem(p + 8 * x_hi, NT)

    def columns(h):
        return pl.ds(pl.multiple_of(h * HD, HD), HD)

    left = (lax.rem(ta + 8 * (1 - core), NT), lax.rem(ha + NH - 1, NH))
    right = (lax.rem(ta + 8 * core, NT), lax.rem(ha + 1, NH))
    sides = (left, right)

    barrier = pltpu.get_barrier_semaphore()

    @pl.loop(1, NT)
    def _(d):
        pl.semaphore_signal(barrier, inc=1, device_id=(peer(d), ha), device_id_type=MESH)

    for side in sides:
        pl.semaphore_signal(barrier, inc=1, device_id=side, device_id_type=MESH)
    pl.semaphore_wait(barrier, NT + 1)

    def remote(src, dst, send_sem, recv_sem, device):
        return pltpu.make_async_remote_copy(
            src_ref=src, dst_ref=dst, send_sem=send_sem, recv_sem=recv_sem,
            device_id=device, device_id_type=MESH,
        )

    def stat_copy(n, d):
        p = peer(d)
        src, dst = ((lse, lse_buf), (delta, delta_buf))[n]
        return remote(src.at[head_of(p)], dst.at[ta], stat_ss.at[n, d], stat_rs.at[n, d], (p, ha))

    def kv_copy(n, d):
        p = peer(d)
        src, dst = ((keys, key_buf), (values, value_buf))[n]
        return remote(
            src.at[:, columns(head_of(p))], dst.at[ta, pl.ds(TOK, TOK), :],
            kv_ss.at[n, d], kv_rs.at[n, d], (p, ha),
        )

    def qg_copy(n, c, d):
        p = peer(d)
        src, dst = ((queries, query_buf), (out_grad, grad_buf))[n]
        return remote(
            src.at[pl.ds(c * HALF, HALF), columns(head_of(p))], dst.at[c, ta],
            qg_ss.at[n, c, d], qg_rs.at[n, c, d], (p, ha),
        )

    own = [
        pltpu.make_async_copy(keys.at[:, columns(head)], key_buf.at[ta, pl.ds(TOK, TOK), :], own_sem.at[0]),
        pltpu.make_async_copy(values.at[:, columns(head)], value_buf.at[ta, pl.ds(TOK, TOK), :], own_sem.at[1]),
        pltpu.make_async_copy(lse.at[head], lse_buf.at[ta], own_sem.at[2]),
        pltpu.make_async_copy(delta.at[head], delta_buf.at[ta], own_sem.at[3]),
    ]
    for c in range(2):
        for n, (src, dst) in enumerate(((queries, query_buf), (out_grad, grad_buf))):
            own.append(
                pltpu.make_async_copy(
                    src.at[pl.ds(c * HALF, HALF), columns(head)], dst.at[c, ta], own_sem.at[4 + 2 * c + n]
                )
            )

    for n in range(2):
        @pl.loop(1, NT)
        def _(d, n=n):
            kv_copy(n, d).start()
    for n in range(2):
        @pl.loop(1, NT)
        def _(d, n=n):
            stat_copy(n, d).start()
    for n in range(2):
        for c in range(2):
            @pl.loop(1, NT)
            def _(d, n=n, c=c):
                qg_copy(n, c, d).start()
    for copy in own:
        copy.start()

    for copy in own:
        copy.wait()

    halos = []
    for n, buf in enumerate((key_buf, value_buf)):
        @pl.loop(1, NT)
        def _(d, n=n):
            kv_copy(n, d).wait_recv()

        for s in range(2):
            copy = remote(
                buf.at[:, pl.ds(TOK, TOK), :],
                buf.at[:, pl.ds(2 * TOK * (1 - s), TOK), :],
                halo_ss.at[n, s], halo_rs.at[n, s], sides[s],
            )
            copy.start()
            halos.append(copy)

    model_head = order[head]

    def pick(at_head):
        entry = at_head(0)
        for m in range(1, NT):
            entry = jnp.where(model_head == m, at_head(m), entry)
        return entry

    def is_early(a):
        return pick(lambda m: time_start[a, m]) == 0

    early = [None] + [is_early(a) for a in (1, 2)]
    low_lane = lax.broadcasted_iota(jnp.int32, (1, HD), 1) < HALF

    def stat_row(buf, a, c):
        rows = [buf[4 * a + i] for i in range(4)]
        flipped = [pltpu.roll(row, HALF, 1) for row in rows]
        if c == 0:
            pairs = [jnp.where(low_lane, rows[2 * i], flipped[2 * i + 1]) for i in range(2)]
        else:
            pairs = [jnp.where(low_lane, flipped[2 * i], rows[2 * i + 1]) for i in range(2)]
        return jnp.concatenate(pairs, axis=1)

    def query_copy(c, frame):
        return remote(
            query_low.at[c, frame], query_out.at[pl.ds(c * HALF, HALF), columns(head)],
            qo_ss.at[c, frame], qo_rs.at[c, ta], (frame, ha),
        )

    def query_own(c):
        return pltpu.make_async_copy(
            query_low.at[c, ta], query_out.at[pl.ds(c * HALF, HALF), columns(head)], qo_ss.at[c, ta]
        )

    steps = [pick(lambda m, c=c: height_start[m, 2 * ha + c]) - (2 * ha + c) + 2 for c in range(2)]
    at = [[step == d for d in range(3)] for step in steps]

    def choose_height(buf, window):
        @pl.loop(0, NT)
        def _(frame):
            for c in range(2):
                spans = [buf[frame, pl.ds(HALF * (c + d), SPAN), :] for d in range(3)]
                window[c, frame] = jnp.where(at[c][0], spans[0], jnp.where(at[c][1], spans[1], spans[2]))

    def tile(window, c, soon, j):
        now = window[c, pl.ds(4 * j, 4)]
        later = window[c, pl.ds(4 * j + 4, 4)]
        return jnp.where(soon, now, later).reshape(4 * SPAN, HD)

    def tokens(buf, c, a):
        return buf[c, pl.ds(4 * a, 4)].reshape(4 * HALF, HD)

    for n in range(2):
        @pl.loop(1, NT)
        def _(d, n=n):
            stat_copy(n, d).wait_recv()

    for s in range(2):
        halos[s].wait_recv()
    choose_height(key_buf, key_window)
    for c in range(2):
        @pl.loop(1, NT)
        def _(d, c=c):
            qg_copy(0, c, d).wait_recv()

        @pl.loop(0, 4)
        def _(a, c=c):
            soon = is_early(a)
            query = tokens(query_buf, c, a)
            lse_row = stat_row(lse_buf, a, c) * LOG2E
            for j in range(3):
                scores = dot(tile(key_window, c, soon, j), query, ((1,), (1,)))
                probs_buf[4 * c + a, j] = jnp.exp2(scores * (SCALE * LOG2E) - lse_row)

    for s in range(2):
        halos[2 + s].wait_recv()
    choose_height(value_buf, value_window)

    def over_time(parts, c):
        @pl.loop(0, 4)
        def _(i):
            def entry(a, j):
                return parts[c, 3 * a + j, i]

            last = jnp.where(early[1], 0.0, entry(1, 2)) + jnp.where(early[2], 0.0, entry(2, 2))
            parts[c, 11, i] = last + entry(3, 2)
            for t in (2, 1):
                found = entry(0, t) + entry(3, t - 1)
                for a in (1, 2):
                    found = found + jnp.where(early[a], entry(a, t), entry(a, t - 1))
                parts[c, 8 + t, i] = found
            first = jnp.where(early[1], entry(1, 0), 0.0) + jnp.where(early[2], entry(2, 0), 0.0)
            parts[c, 0, i] = first + entry(0, 0)

    def piece(parts, frame, c, e):
        t = frame // 4
        place = jnp.where(t == 0, 0, 8 + t)
        found = None
        for d in range(3):
            k = e - c - d
            if 0 <= k < 3:
                got = parts[c, place, lax.rem(frame, 4), HALF * k : HALF * (k + 1), :]
                found = jnp.where(at[c][d], got, 0.0 if found is None else found)
        return found

    def around(parts, frame, e):
        found = [piece(parts, frame, c, e) for c in range(2) if 0 <= e - c < 5]
        return found[0] if len(found) == 1 else found[0] + found[1]

    back = {}

    def send_back(n, e):
        parts, send, recv = ((key_parts, key_send, key_recv), (value_parts, value_send, value_recv))[n]
        s, c = e // 4, e % 2

        @pl.loop(0, NT)
        def _(frame):
            send[s, c, frame] = around(parts, frame, e).astype(jnp.bfloat16)

        copy = remote(
            send.at[s, c], recv.at[1 - s, c], back_ss.at[n, c, s], back_rs.at[n, c, 1 - s], sides[s]
        )
        copy.start()
        back[n, c, s] = copy

    for c in range(2):
        @pl.loop(1, NT)
        def _(d, c=c):
            qg_copy(1, c, d).wait_recv()

        @pl.loop(0, 4)
        def _(a, c=c):
            soon = is_early(a)
            query = tokens(query_buf, c, a)
            grad = tokens(grad_buf, c, a)
            delta_row = stat_row(delta_buf, a, c)
            turned = jnp.zeros((HD, 4 * HALF), jnp.float32)
            for j in range(3):
                key = tile(key_window, c, soon, j)
                value = tile(value_window, c, soon, j)
                probs = probs_buf[4 * c + a, j]
                dprob = dot(value, grad, ((1,), (1,)))
                dscore = (probs * (dprob - delta_row)).astype(jnp.bfloat16)
                value_parts[c, 3 * a + j] = dot(
                    probs.astype(jnp.bfloat16), grad, ((1,), (0,))
                ).reshape(4, SPAN, HD)
                key_parts[c, 3 * a + j] = dot(dscore, query, ((1,), (0,))).reshape(4, SPAN, HD)
                turned = turned + dot(key, dscore, ((0,), (0,)))
            query_low[c, pl.ds(4 * a, 4)] = (
                (turned.T * SCALE).astype(jnp.bfloat16).reshape(4, HALF, HD)
            )
            for i in range(4):
                frame = 4 * a + i

                @pl.when(frame != ta)
                def _(frame=frame):
                    query_copy(c, frame).start()

                @pl.when(frame == ta)
                def _():
                    query_own(c).start()

        over_time(value_parts, c)
        if c == 0:
            over_time(key_parts, c)
            send_back(1, 0)
            send_back(0, 0)

    send_back(1, 4)
    send_back(1, 1)
    send_back(1, 5)
    over_time(key_parts, 1)
    send_back(0, 4)
    send_back(0, 1)
    send_back(0, 5)

    def grad_copy(n, c, d):
        p = peer(d)
        low, out = ((key_low, key_out), (value_low, value_out))[n]
        return remote(
            low.at[c, p], out.at[pl.ds(c * HALF, HALF), columns(head)],
            kvo_ss.at[n, c, d], kvo_rs.at[n, c, d], (p, ha),
        )

    own_out = []
    for n in (1, 0):
        parts, recv, low, out = (
            (key_parts, key_recv, key_low, key_out), (value_parts, value_recv, value_low, value_out)
        )[n]
        factor = SCALE if n == 0 else 1.0
        for c in range(2):
            for s in range(2):
                back[n, c, s].wait_recv()

            @pl.loop(0, NT)
            def _(frame, parts=parts, recv=recv, low=low, factor=factor, c=c):
                whole = (
                    around(parts, frame, 2 + c)
                    + recv[0, c, frame].astype(jnp.float32)
                    + recv[1, c, frame].astype(jnp.float32)
                )
                low[c, frame] = (whole * factor).astype(jnp.bfloat16)

            @pl.loop(1, NT)
            def _(d, n=n, c=c):
                grad_copy(n, c, d).start()

            copy = pltpu.make_async_copy(
                low.at[c, ta], out.at[pl.ds(c * HALF, HALF), columns(head)], own_sem.at[2 * n + c]
            )
            copy.start()
            own_out.append(copy)

    for n in range(2):
        @pl.loop(1, NT)
        def _(d, n=n):
            stat_copy(n, d).wait_send()
            kv_copy(n, d).wait_send()
            for c in range(2):
                qg_copy(n, c, d).wait_send()
    for copy in halos + list(back.values()):
        copy.wait_send()
    for c in range(2):
        query_own(c).wait()

        @pl.loop(1, NT)
        def _(d, c=c):
            frame = peer(d)
            done = remote(
                query_low.at[c, frame], query_out.at[pl.ds(c * HALF, HALF), columns(head_of(frame))],
                qo_ss.at[c, frame], qo_rs.at[c, frame], (frame, ha),
            )
            done.wait_send()
            done.wait_recv()

    for n in range(2):
        for c in range(2):
            @pl.loop(1, NT)
            def _(d, n=n, c=c):
                grad_copy(n, c, d).wait()

    for copy in own_out:
        copy.wait()


def move_kernel(*refs):
    sources, targets, buf, in_sem, out_sem = refs[:3], refs[3:6], refs[6], refs[7], refs[8]
    rows = [pl.ds(c * HALF, HALF) for c in range(2)]
    arrive = [
        pltpu.make_async_copy(sources[i].at[rows[c]], buf.at[i, rows[c]], in_sem.at[i, c])
        for i in range(3) for c in range(2)
    ]
    leave = [
        pltpu.make_async_copy(buf.at[i, rows[c]], targets[i].at[rows[c]], out_sem.at[i, c])
        for i in range(3) for c in range(2)
    ]
    for copy in arrive:
        copy.start()
    for first, second in zip(arrive, leave):
        first.wait()
        second.start()
    for copy in leave:
        copy.wait()


def per_device(
    queries, keys, values, out_grad, log_sum_exp, row_delta, time_start, height_start, head_order
):
    width = NT * HD
    flat = [x.reshape(TOK, width) for x in (queries, keys, values, out_grad)]
    smem = pl.BlockSpec(memory_space=pltpu.SMEM)
    hbm = pl.BlockSpec(memory_space=pl.ANY)
    bf16, f32 = jnp.bfloat16, jnp.float32
    dma = pltpu.SemaphoreType.DMA
    outs = pl.pallas_call(
        grads_kernel,
        name="tile_attention_grads",
        out_shape=[jax.ShapeDtypeStruct((TOK, width), bf16)] * 3,
        in_specs=[smem] * 3 + [hbm] * 6,
        out_specs=[hbm] * 3,
        scratch_shapes=[
            pltpu.VMEM((NT, 3 * TOK, HD), bf16),
            pltpu.VMEM((NT, 3 * TOK, HD), bf16),
            pltpu.VMEM((2, NT, HALF, HD), bf16),
            pltpu.VMEM((2, NT, HALF, HD), bf16),
            pltpu.VMEM((NT, 1, TOK), f32),
            pltpu.VMEM((NT, 1, TOK), f32),
            pltpu.VMEM((2, NT, SPAN, HD), bf16),
            pltpu.VMEM((2, NT, SPAN, HD), bf16),
            pltpu.VMEM((8, 3, 4 * SPAN, 4 * HALF), f32),
            pltpu.VMEM((2, 12, 4, SPAN, HD), f32),
            pltpu.VMEM((2, 12, 4, SPAN, HD), f32),
            pltpu.VMEM((2, NT, HALF, HD), bf16),
            pltpu.VMEM((2, NT, HALF, HD), bf16),
            pltpu.VMEM((2, NT, HALF, HD), bf16),
            pltpu.VMEM((2, 2, NT, HALF, HD), bf16),
            pltpu.VMEM((2, 2, NT, HALF, HD), bf16),
            pltpu.VMEM((2, 2, NT, HALF, HD), bf16),
            pltpu.VMEM((2, 2, NT, HALF, HD), bf16),
            dma((2, NT)), dma((2, NT)),
            dma((2, NT)), dma((2, NT)),
            dma((2, 2, NT)), dma((2, 2, NT)),
            dma((8,)),
            dma((2, 2)), dma((2, 2)),
            dma((2, 2, 2)), dma((2, 2, 2)),
            dma((2, NT)), dma((2, NT)),
            dma((2, 2, NT)), dma((2, 2, NT)),
        ],
        compiler_params=pltpu.CompilerParams(
            collective_id=0, has_side_effects=True, vmem_limit_bytes=60 * 2**20
        ),
    )(head_order, time_start.T, height_start, log_sum_exp, row_delta, *flat)
    outs = pl.pallas_call(
        move_kernel,
        name="place_grads",
        out_shape=[jax.ShapeDtypeStruct((TOK, width), bf16)] * 3,
        in_specs=[hbm] * 3,
        out_specs=[hbm] * 3,
        scratch_shapes=[pltpu.VMEM((3, TOK, width), bf16), dma((3, 2)), dma((3, 2))],
        compiler_params=pltpu.CompilerParams(vmem_limit_bytes=60 * 2**20),
    )(*outs)
    return tuple(x.reshape(queries.shape) for x in outs)


def solution(mesh):
    rows = P("ta", "ha", None, None)
    stats = P(None, "ta", "ha")
    return jax.shard_map(
        per_device,
        mesh=mesh,
        in_specs=(rows, rows, rows, rows, stats, stats, P(), P(), P()),
        out_specs=(rows, rows, rows),
        check_vma=False,
    )
```

time: 118 us -> 109 us (0.924)
  local copies, waits for them, and re-layouts: 5.32 us -> 0 us
  Pallas kernels: 111 us -> 108 us
    pallas_call x1, Pallas kernels: 111 us -> 106 us  [per_device(): pl.pallas_call(grads_kernel, name='tile_attention_grads', out_shape=[jax....]
    unnamed x10 -> x0, local copies, waits for them, and re-layouts: 5.32 us -> none
    pallas_call x0 -> x1, Pallas kernels: none -> 2.19 us  [per_device(): pl.pallas_call(move_kernel, name='place_grads', out_shape=[jax.ShapeDtype...]
where the time goes in v2:
time: 109 us
  Pallas kernels  108 us (99%)
    pallas_call x1, Pallas kernels, per_device(): pl.pallas_call(grads_kernel, name='tile_attention_grads', out_shape=[jax....  106 us
    pallas_call x1, Pallas kernels, per_device(): pl.pallas_call(move_kernel, name='place_grads', out_shape=[jax.ShapeDtype...  2.19 us

profile of v2, /device:TPU:1, one launch (start us, length us, event | category | flops | bytes accessed | tf_op | source)
XLA Modules:
  0.0 108.7 jit_solution(16472699415343710897)
XLA Ops:
  0.6 105.9 %tile_attention_grads.1 = (bf16[128,2048]{1,0:T(8,128)(2,1)}, bf16[128,2048]{1,0:T(8,128)(2,1)}, bf16[128,2048]{1,0:T(8,128)(2,1)}) custom-call(s32[16]{0:T(128)} %order.1, s32[4,16]{1,0:T(4,128)} %bitcast.12, s32[16,64]{1,0:T(8,128)} %height_start.1, f32[16,1,128]{2,1,0:T(1,128)} %lse.1, f32[16,1,128]{2,1,0:T(1,128)} %delta.1, bf16[128,2048]{1,0:T(8,128)(2,1)} %bitcast.8, ...), custom_call_target="tpu_custom_call" | custom-call | tf_op jit(solution)/shard_map/tile_attention_grads/pallas_call | solution.py:413
  106.5 2.2 %place_grads.1 = (bf16[128,2048]{1,0:T(8,128)(2,1)}, bf16[128,2048]{1,0:T(8,128)(2,1)}, bf16[128,2048]{1,0:T(8,128)(2,1)}) custom-call(bf16[128,2048]{1,0:T(8,128)(2,1)} %get-tuple-element.9.refs_0_, bf16[128,2048]{1,0:T(8,128)(2,1)} %get-tuple-element.10.refs_1_, bf16[128,2048]{1,0:T(8,128)(2,1)} %get-tuple-element.11.refs_2_), custom_call_target="tpu_custom_call" | custom-call | tf_op jit(solution)/shard_map/place_grads/pallas_call | solution.py:451

commit v3 on v2

v3 whole, which is shorter than its diff:
```python
import functools

import jax
import jax.numpy as jnp
from jax import lax
from jax.experimental import pallas as pl
from jax.experimental.pallas import tpu as pltpu
from jax.sharding import PartitionSpec as P

HD = 128
SCALE = HD ** -0.5
LOG2E = 1.4426950408889634
NT = 16
NH = 32
TOK = 128
HALF = 64
SPAN = 3 * HALF
MESH = pl.DeviceIdType.MESH


def dot(a, b, dims):
    return lax.dot_general(a, b, (dims, ((), ())), preferred_element_type=jnp.float32)


def grads_kernel(
    order, time_start, height_start, lse, delta, queries, keys, values, out_grad,
    query_out, key_out, value_out,
    key_buf, value_buf, query_buf, grad_buf, lse_buf, delta_buf,
    key_window, value_window, probs_buf, key_parts, value_parts,
    query_low, key_low, value_low,
    key_send, value_send, key_recv, value_recv,
    stat_ss, stat_rs, kv_ss, kv_rs, qg_ss, qg_rs, own_sem,
    halo_ss, halo_rs, back_ss, back_rs, qo_ss, qo_rs, kvo_ss, kvo_rs,
):
    ta = lax.axis_index("ta")
    ha = lax.axis_index("ha")
    core = lax.rem(ha, 2)
    x_hi = lax.rem(ha // 2, 2)
    head = lax.rem(ta + 8 * x_hi, NT)

    def peer(d):
        return lax.rem(ta + d, NT)

    def head_of(p):
        return lax.rem(p + 8 * x_hi, NT)

    def columns(h):
        return pl.ds(pl.multiple_of(h * HD, HD), HD)

    left = (lax.rem(ta + 8 * (1 - core), NT), lax.rem(ha + NH - 1, NH))
    right = (lax.rem(ta + 8 * core, NT), lax.rem(ha + 1, NH))
    sides = (left, right)
    across = (lax.rem(ta + 8, NT), lax.rem(ha + NH - 1 + 2 * core, NH))
    within = (ta, ha + 1 - 2 * core)
    spot = (core, 1 - core)

    def rows_of(k):
        return pl.ds(pl.multiple_of(spot[k] * HALF, HALF), HALF)

    barrier = pltpu.get_barrier_semaphore()

    @pl.loop(1, NT)
    def _(d):
        pl.semaphore_signal(barrier, inc=1, device_id=(peer(d), ha), device_id_type=MESH)

    for side in sides:
        pl.semaphore_signal(barrier, inc=1, device_id=side, device_id_type=MESH)
    pl.semaphore_wait(barrier, NT + 1)

    def remote(src, dst, send_sem, recv_sem, device):
        return pltpu.make_async_remote_copy(
            src_ref=src, dst_ref=dst, send_sem=send_sem, recv_sem=recv_sem,
            device_id=device, device_id_type=MESH,
        )

    def stat_copy(n, d):
        p = peer(d)
        src, dst = ((lse, lse_buf), (delta, delta_buf))[n]
        return remote(src.at[head_of(p)], dst.at[ta], stat_ss.at[n, d], stat_rs.at[n, d], (p, ha))

    def kv_copy(n, d):
        p = peer(d)
        src, dst = ((keys, key_buf), (values, value_buf))[n]
        return remote(
            src.at[:, columns(head_of(p))], dst.at[ta, pl.ds(TOK, TOK), :],
            kv_ss.at[n, d], kv_rs.at[n, d], (p, ha),
        )

    def qg_copy(n, k, d):
        p = peer(d)
        src, dst = ((queries, query_buf), (out_grad, grad_buf))[n]
        return remote(
            src.at[rows_of(k), columns(head_of(p))], dst.at[k, ta],
            qg_ss.at[n, k, d], qg_rs.at[n, k, d], (p, ha),
        )

    own = [
        pltpu.make_async_copy(keys.at[:, columns(head)], key_buf.at[ta, pl.ds(TOK, TOK), :], own_sem.at[0]),
        pltpu.make_async_copy(values.at[:, columns(head)], value_buf.at[ta, pl.ds(TOK, TOK), :], own_sem.at[1]),
        pltpu.make_async_copy(lse.at[head], lse_buf.at[ta], own_sem.at[2]),
        pltpu.make_async_copy(delta.at[head], delta_buf.at[ta], own_sem.at[3]),
    ]
    for k in range(2):
        for n, (src, dst) in enumerate(((queries, query_buf), (out_grad, grad_buf))):
            own.append(
                pltpu.make_async_copy(src.at[rows_of(k), columns(head)], dst.at[k, ta], own_sem.at[4 + 2 * k + n])
            )

    for n in range(2):
        @pl.loop(1, NT)
        def _(d, n=n):
            kv_copy(n, d).start()
    for n in range(2):
        @pl.loop(1, NT)
        def _(d, n=n):
            stat_copy(n, d).start()
    for k in range(2):
        for n in range(2):
            @pl.loop(1, NT)
            def _(d, n=n, k=k):
                qg_copy(n, k, d).start()
    for copy in own:
        copy.start()

    for copy in own:
        copy.wait()

    halos = []
    for n, buf in enumerate((key_buf, value_buf)):
        @pl.loop(1, NT)
        def _(d, n=n):
            kv_copy(n, d).wait_recv()

        for s in range(2):
            copy = remote(
                buf.at[:, pl.ds(TOK, TOK), :],
                buf.at[:, pl.ds(2 * TOK * (1 - s), TOK), :],
                halo_ss.at[n, s], halo_rs.at[n, s], sides[s],
            )
            copy.start()
            halos.append(copy)

    model_head = order[head]

    def pick(at_head):
        entry = at_head(0)
        for m in range(1, NT):
            entry = jnp.where(model_head == m, at_head(m), entry)
        return entry

    def is_early(a):
        return pick(lambda m: time_start[a, m]) == 0

    early = [None] + [is_early(a) for a in (1, 2)]
    low_lane = lax.broadcasted_iota(jnp.int32, (1, HD), 1) < HALF

    def stat_row(buf, a, k):
        rows = [buf[4 * a + i] for i in range(4)]
        flipped = [pltpu.roll(row, HALF, 1) for row in rows]
        low = spot[k] == 0
        pairs = [
            jnp.where(
                low_lane,
                jnp.where(low, rows[2 * i], flipped[2 * i]),
                jnp.where(low, flipped[2 * i + 1], rows[2 * i + 1]),
            )
            for i in range(2)
        ]
        return jnp.concatenate(pairs, axis=1)

    def query_copy(k, frame):
        return remote(
            query_low.at[k, frame], query_out.at[rows_of(k), columns(head)],
            qo_ss.at[k, frame], qo_rs.at[k, ta], (frame, ha),
        )

    def query_own(k):
        return pltpu.make_async_copy(
            query_low.at[k, ta], query_out.at[rows_of(k), columns(head)], qo_ss.at[k, ta]
        )

    steps = [pick(lambda m, k=k: height_start[m, 2 * ha + spot[k]]) - (2 * ha + spot[k]) + 2 for k in range(2)]
    starts = [[step == d for d in range(3)] for step in steps]
    at = [[jnp.where(core == 0, step, 2 - step) == d for d in range(3)] for step in steps]

    def choose_height(buf, window):
        @pl.loop(0, NT)
        def _(frame):
            for k in range(2):
                spans = [
                    buf[frame, pl.ds(pl.multiple_of(HALF * (spot[k] + d), HALF), SPAN), :] for d in range(3)
                ]
                window[k, frame] = jnp.where(
                    starts[k][0], spans[0], jnp.where(starts[k][1], spans[1], spans[2])
                )

    def tile(window, k, soon, j):
        now = window[k, pl.ds(4 * j, 4)]
        later = window[k, pl.ds(4 * j + 4, 4)]
        return jnp.where(soon, now, later).reshape(4 * SPAN, HD)

    def tokens(buf, k, a):
        return buf[k, pl.ds(4 * a, 4)].reshape(4 * HALF, HD)

    def probabilities(k):
        @pl.loop(1, NT)
        def _(d):
            qg_copy(0, k, d).wait_recv()

        @pl.loop(0, 4)
        def _(a):
            soon = is_early(a)
            query = tokens(query_buf, k, a)
            lse_row = stat_row(lse_buf, a, k) * LOG2E
            for j in range(3):
                scores = dot(tile(key_window, k, soon, j), query, ((1,), (1,)))
                probs_buf[a, j] = jnp.exp2(scores * (SCALE * LOG2E) - lse_row)

    def gradients(k):
        @pl.loop(1, NT)
        def _(d):
            qg_copy(1, k, d).wait_recv()

        @pl.loop(0, 4)
        def _(a):
            soon = is_early(a)
            query = tokens(query_buf, k, a)
            grad = tokens(grad_buf, k, a)
            delta_row = stat_row(delta_buf, a, k)
            turned = jnp.zeros((HD, 4 * HALF), jnp.float32)
            for j in range(3):
                key = tile(key_window, k, soon, j)
                value = tile(value_window, k, soon, j)
                probs = probs_buf[a, j]
                dprob = dot(value, grad, ((1,), (1,)))
                dscore = (probs * (dprob - delta_row)).astype(jnp.bfloat16)
                value_parts[k, 3 * a + j] = dot(
                    probs.astype(jnp.bfloat16), grad, ((1,), (0,))
                ).reshape(4, SPAN, HD)
                key_parts[k, 3 * a + j] = dot(dscore, query, ((1,), (0,))).reshape(4, SPAN, HD)
                turned = turned + dot(key, dscore, ((0,), (0,)))
            query_low[k, pl.ds(4 * a, 4)] = (
                (turned.T * SCALE).astype(jnp.bfloat16).reshape(4, HALF, HD)
            )
            for i in range(4):
                frame = 4 * a + i

                @pl.when(frame != ta)
                def _(frame=frame):
                    query_copy(k, frame).start()

                @pl.when(frame == ta)
                def _():
                    query_own(k).start()

    def over_time(parts, k):
        @pl.loop(0, 4)
        def _(i):
            def entry(a, j):
                return parts[k, 3 * a + j, i]

            last = jnp.where(early[1], 0.0, entry(1, 2)) + jnp.where(early[2], 0.0, entry(2, 2))
            parts[k, 11, i] = last + entry(3, 2)
            for t in (2, 1):
                found = entry(0, t) + entry(3, t - 1)
                for a in (1, 2):
                    found = found + jnp.where(early[a], entry(a, t), entry(a, t - 1))
                parts[k, 8 + t, i] = found
            first = jnp.where(early[1], entry(1, 0), 0.0) + jnp.where(early[2], entry(2, 0), 0.0)
            parts[k, 0, i] = first + entry(0, 0)

    def piece(parts, frame, k, e):
        t = frame // 4
        place = jnp.where(t == 0, 0, 8 + t)
        found = None
        for d in range(3):
            w = e - k - d
            if 0 <= w < 3:
                spot_w = pl.multiple_of(HALF * (w + core * (2 - 2 * w)), HALF)
                got = parts[k, place, lax.rem(frame, 4), pl.ds(spot_w, HALF), :]
                found = jnp.where(at[k][d], got, 0.0 if found is None else found)
        return found

    def around(parts, frame, e):
        found = [piece(parts, frame, k, e) for k in range(2) if 0 <= e - k < 5]
        return found[0] if len(found) == 1 else found[0] + found[1]

    back = {}

    def send_back(n, e):
        parts, send, recv = ((key_parts, key_send, key_recv), (value_parts, value_send, value_recv))[n]
        s, k = e // 4, (e + 1) % 2

        @pl.loop(0, NT)
        def _(frame):
            send[s, k, frame] = around(parts, frame, e).astype(jnp.bfloat16)

        copy = remote(
            send.at[s, k], recv.at[s, k], back_ss.at[n, k, s], back_rs.at[n, k, s], (across, within)[s]
        )
        copy.start()
        back[n, k, s] = copy

    for n in range(2):
        @pl.loop(1, NT)
        def _(d, n=n):
            stat_copy(n, d).wait_recv()

    for s in range(2):
        halos[s].wait_recv()
    choose_height(key_buf, key_window)
    probabilities(0)
    for s in range(2):
        halos[2 + s].wait_recv()
    choose_height(value_buf, value_window)
    gradients(0)
    for n in (1, 0):
        over_time((key_parts, value_parts)[n], 0)
        send_back(n, 0)
    probabilities(1)
    gradients(1)
    for n in (1, 0):
        over_time((key_parts, value_parts)[n], 1)
        send_back(n, 4)
    for e in (1, 5):
        for n in (1, 0):
            send_back(n, e)

    def grad_copy(n, k, d):
        p = peer(d)
        low, out = ((key_low, key_out), (value_low, value_out))[n]
        return remote(
            low.at[k, p], out.at[rows_of(k), columns(head)],
            kvo_ss.at[n, k, d], kvo_rs.at[n, k, d], (p, ha),
        )

    own_out = []
    for k in (1, 0):
        for n in (1, 0):
            parts, recv, low, out = (
                (key_parts, key_recv, key_low, key_out), (value_parts, value_recv, value_low, value_out)
            )[n]
            factor = SCALE if n == 0 else 1.0
            for s in range(2):
                back[n, k, s].wait_recv()

            @pl.loop(0, NT)
            def _(frame, parts=parts, recv=recv, low=low, factor=factor, k=k):
                whole = (
                    around(parts, frame, 2 + k)
                    + recv[0, k, frame].astype(jnp.float32)
                    + recv[1, k, frame].astype(jnp.float32)
                )
                low[k, frame] = (whole * factor).astype(jnp.bfloat16)

            @pl.loop(1, NT)
            def _(d, n=n, k=k):
                grad_copy(n, k, d).start()

            copy = pltpu.make_async_copy(
                low.at[k, ta], out.at[rows_of(k), columns(head)], own_sem.at[2 * n + k]
            )
            copy.start()
            own_out.append(copy)

    for n in range(2):
        @pl.loop(1, NT)
        def _(d, n=n):
            stat_copy(n, d).wait_send()
            kv_copy(n, d).wait_send()
            for k in range(2):
                qg_copy(n, k, d).wait_send()
    for copy in halos + list(back.values()):
        copy.wait_send()
    for k in range(2):
        query_own(k).wait()

        @pl.loop(1, NT)
        def _(d, k=k):
            frame = peer(d)
            done = remote(
                query_low.at[k, frame], query_out.at[rows_of(k), columns(head_of(frame))],
                qo_ss.at[k, frame], qo_rs.at[k, frame], (frame, ha),
            )
            done.wait_send()
            done.wait_recv()

    for n in range(2):
        for k in range(2):
            @pl.loop(1, NT)
            def _(d, n=n, k=k):
                grad_copy(n, k, d).wait()

    for copy in own_out:
        copy.wait()


def move_kernel(*refs):
    sources, targets, buf, in_sem, out_sem = refs[:3], refs[3:6], refs[6], refs[7], refs[8]
    rows = [pl.ds(c * HALF, HALF) for c in range(2)]
    arrive = [
        pltpu.make_async_copy(sources[i].at[rows[c]], buf.at[i, rows[c]], in_sem.at[i, c])
        for i in range(3) for c in range(2)
    ]
    leave = [
        pltpu.make_async_copy(buf.at[i, rows[c]], targets[i].at[rows[c]], out_sem.at[i, c])
        for i in range(3) for c in range(2)
    ]
    for copy in arrive:
        copy.start()
    for first, second in zip(arrive, leave):
        first.wait()
        second.start()
    for copy in leave:
        copy.wait()


def per_device(
    queries, keys, values, out_grad, log_sum_exp, row_delta, time_start, height_start, head_order
):
    width = NT * HD
    flat = [x.reshape(TOK, width) for x in (queries, keys, values, out_grad)]
    smem = pl.BlockSpec(memory_space=pltpu.SMEM)
    hbm = pl.BlockSpec(memory_space=pl.ANY)
    bf16, f32 = jnp.bfloat16, jnp.float32
    dma = pltpu.SemaphoreType.DMA
    outs = pl.pallas_call(
        grads_kernel,
        name="tile_attention_grads",
        out_shape=[jax.ShapeDtypeStruct((TOK, width), bf16)] * 3,
        in_specs=[smem] * 3 + [hbm] * 6,
        out_specs=[hbm] * 3,
        scratch_shapes=[
            pltpu.VMEM((NT, 3 * TOK, HD), bf16),
            pltpu.VMEM((NT, 3 * TOK, HD), bf16),
            pltpu.VMEM((2, NT, HALF, HD), bf16),
            pltpu.VMEM((2, NT, HALF, HD), bf16),
            pltpu.VMEM((NT, 1, TOK), f32),
            pltpu.VMEM((NT, 1, TOK), f32),
            pltpu.VMEM((2, NT, SPAN, HD), bf16),
            pltpu.VMEM((2, NT, SPAN, HD), bf16),
            pltpu.VMEM((4, 3, 4 * SPAN, 4 * HALF), f32),
            pltpu.VMEM((2, 12, 4, SPAN, HD), f32),
            pltpu.VMEM((2, 12, 4, SPAN, HD), f32),
            pltpu.VMEM((2, NT, HALF, HD), bf16),
            pltpu.VMEM((2, NT, HALF, HD), bf16),
            pltpu.VMEM((2, NT, HALF, HD), bf16),
            pltpu.VMEM((2, 2, NT, HALF, HD), bf16),
            pltpu.VMEM((2, 2, NT, HALF, HD), bf16),
            pltpu.VMEM((2, 2, NT, HALF, HD), bf16),
            pltpu.VMEM((2, 2, NT, HALF, HD), bf16),
            dma((2, NT)), dma((2, NT)),
            dma((2, NT)), dma((2, NT)),
            dma((2, 2, NT)), dma((2, 2, NT)),
            dma((8,)),
            dma((2, 2)), dma((2, 2)),
            dma((2, 2, 2)), dma((2, 2, 2)),
            dma((2, NT)), dma((2, NT)),
            dma((2, 2, NT)), dma((2, 2, NT)),
        ],
        compiler_params=pltpu.CompilerParams(
            collective_id=0, has_side_effects=True, vmem_limit_bytes=60 * 2**20
        ),
    )(head_order, time_start.T, height_start, log_sum_exp, row_delta, *flat)
    outs = pl.pallas_call(
        move_kernel,
        name="place_grads",
        out_shape=[jax.ShapeDtypeStruct((TOK, width), bf16)] * 3,
        in_specs=[hbm] * 3,
        out_specs=[hbm] * 3,
        scratch_shapes=[pltpu.VMEM((3, TOK, width), bf16), dma((3, 2)), dma((3, 2))],
        compiler_params=pltpu.CompilerParams(vmem_limit_bytes=60 * 2**20),
    )(*outs)
    return tuple(x.reshape(queries.shape) for x in outs)


def solution(mesh):
    rows = P("ta", "ha", None, None)
    stats = P(None, "ta", "ha")
    return jax.shard_map(
        per_device,
        mesh=mesh,
        in_specs=(rows, rows, rows, rows, stats, stats, P(), P(), P()),
        out_specs=(rows, rows, rows),
        check_vma=False,
    )
```

time: 109 us -> 107 us (0.982)
  Pallas kernels: 108 us -> 106 us
    pallas_call x1, Pallas kernels: 106 us -> 103 us  [per_device(): pl.pallas_call(grads_kernel, name='tile_attention_grads', out_shape=[jax....]
where the time goes in v3:
time: 107 us; the launch traced here: 106 us
  Pallas kernels  106 us (99%)
    pallas_call x1, Pallas kernels, per_device(): pl.pallas_call(grads_kernel, name='tile_attention_grads', out_shape=[jax....  103 us
    pallas_call x1, Pallas kernels, per_device(): pl.pallas_call(move_kernel, name='place_grads', out_shape=[jax.ShapeDtype...  2.19 us

profile of v3, /device:TPU:1, one launch (start us, length us, event | category | flops | bytes accessed | tf_op | source)
XLA Modules:
  0.0 106.3 jit_solution(6330255199377028268)
XLA Ops:
  0.6 103.5 %tile_attention_grads.1 = (bf16[128,2048]{1,0:T(8,128)(2,1)}, bf16[128,2048]{1,0:T(8,128)(2,1)}, bf16[128,2048]{1,0:T(8,128)(2,1)}) custom-call(s32[16]{0:T(128)} %order.1, s32[4,16]{1,0:T(4,128)} %bitcast.12, s32[16,64]{1,0:T(8,128)} %height_start.1, f32[16,1,128]{2,1,0:T(1,128)} %lse.1, f32[16,1,128]{2,1,0:T(1,128)} %delta.1, bf16[128,2048]{1,0:T(8,128)(2,1)} %bitcast.8, ...), custom_call_target="tpu_custom_call" | custom-call | tf_op jit(solution)/shard_map/tile_attention_grads/pallas_call | solution.py:427
  104.1 2.2 %place_grads.1 = (bf16[128,2048]{1,0:T(8,128)(2,1)}, bf16[128,2048]{1,0:T(8,128)(2,1)}, bf16[128,2048]{1,0:T(8,128)(2,1)}) custom-call(bf16[128,2048]{1,0:T(8,128)(2,1)} %get-tuple-element.9.refs_0_, bf16[128,2048]{1,0:T(8,128)(2,1)} %get-tuple-element.10.refs_1_, bf16[128,2048]{1,0:T(8,128)(2,1)} %get-tuple-element.11.refs_2_), custom_call_target="tpu_custom_call" | custom-call | tf_op jit(solution)/shard_map/place_grads/pallas_call | solution.py:465

commit v4 on v3

--- a/solution.py
+++ b/solution.py
@@ -24,10 +24,10 @@
 
 def grads_kernel(
     order, time_start, height_start, lse, delta, queries, keys, values, out_grad,
-    query_out, key_out, value_out,
-    key_buf, value_buf, query_buf, grad_buf, lse_buf, delta_buf,
+    query_out, pair_out,
+    qg_stage, stat_stage, key_buf, value_buf, qg_buf, stat_buf,
     key_window, value_window, probs_buf, key_parts, value_parts,
-    query_low, key_low, value_low,
+    query_low, pair_low, inner_low,
     key_send, value_send, key_recv, value_recv,
     stat_ss, stat_rs, kv_ss, kv_rs, qg_ss, qg_rs, own_sem,
     halo_ss, halo_rs, back_ss, back_rs, qo_ss, qo_rs, kvo_ss, kvo_rs,
@@ -73,10 +73,9 @@
             device_id=device, device_id_type=MESH,
         )
 
-    def stat_copy(n, d):
+    def stat_copy(d):
         p = peer(d)
-        src, dst = ((lse, lse_buf), (delta, delta_buf))[n]
-        return remote(src.at[head_of(p)], dst.at[ta], stat_ss.at[n, d], stat_rs.at[n, d], (p, ha))
+        return remote(stat_stage.at[head_of(p)], stat_buf.at[ta], stat_ss.at[d], stat_rs.at[d], (p, ha))
 
     def kv_copy(n, d):
         p = peer(d)
@@ -86,42 +85,52 @@
             kv_ss.at[n, d], kv_rs.at[n, d], (p, ha),
         )
 
-    def qg_copy(n, k, d):
+    def qg_copy(k, d):
         p = peer(d)
-        src, dst = ((queries, query_buf), (out_grad, grad_buf))[n]
         return remote(
-            src.at[rows_of(k), columns(head_of(p))], dst.at[k, ta],
-            qg_ss.at[n, k, d], qg_rs.at[n, k, d], (p, ha),
-        )
-
-    own = [
-        pltpu.make_async_copy(keys.at[:, columns(head)], key_buf.at[ta, pl.ds(TOK, TOK), :], own_sem.at[0]),
-        pltpu.make_async_copy(values.at[:, columns(head)], value_buf.at[ta, pl.ds(TOK, TOK), :], own_sem.at[1]),
-        pltpu.make_async_copy(lse.at[head], lse_buf.at[ta], own_sem.at[2]),
-        pltpu.make_async_copy(delta.at[head], delta_buf.at[ta], own_sem.at[3]),
+            qg_stage.at[k, :, :, columns(head_of(p))], qg_buf.at[k, ta],
+            qg_ss.at[k, d], qg_rs.at[k, d], (p, ha),
+        )
+
+    staged = [
+        pltpu.make_async_copy(src, stat_stage.at[:, n], own_sem.at[n]) for n, src in enumerate((lse, delta))
     ]
     for k in range(2):
-        for n, (src, dst) in enumerate(((queries, query_buf), (out_grad, grad_buf))):
-            own.append(
-                pltpu.make_async_copy(src.at[rows_of(k), columns(head)], dst.at[k, ta], own_sem.at[4 + 2 * k + n])
-            )
+        for n, src in enumerate((queries, out_grad)):
+            staged.append(pltpu.make_async_copy(src.at[rows_of(k), :], qg_stage.at[k, n], own_sem.at[2 + 2 * k + n]))
+    for copy in staged:
+        copy.start()
 
     for n in range(2):
         @pl.loop(1, NT)
         def _(d, n=n):
             kv_copy(n, d).start()
-    for n in range(2):
-        @pl.loop(1, NT)
-        def _(d, n=n):
-            stat_copy(n, d).start()
-    for k in range(2):
-        for n in range(2):
-            @pl.loop(1, NT)
-            def _(d, n=n, k=k):
-                qg_copy(n, k, d).start()
+
+    own = [
+        pltpu.make_async_copy(keys.at[:, columns(head)], key_buf.at[ta, pl.ds(TOK, TOK), :], own_sem.at[6]),
+        pltpu.make_async_copy(values.at[:, columns(head)], value_buf.at[ta, pl.ds(TOK, TOK), :], own_sem.at[7]),
+    ]
     for copy in own:
         copy.start()
-
+    for copy in staged:
+        copy.wait()
+
+    @pl.loop(1, NT)
+    def _(d):
+        stat_copy(d).start()
+
+    for k in range(2):
+        @pl.loop(1, NT)
+        def _(d, k=k):
+            qg_copy(k, d).start()
+
+    own.append(pltpu.make_async_copy(stat_stage.at[head], stat_buf.at[ta], own_sem.at[0]))
+    for k in range(2):
+        own.append(
+            pltpu.make_async_copy(qg_stage.at[k, :, :, columns(head)], qg_buf.at[k, ta], own_sem.at[1 + k])
+        )
+    for copy in own[2:]:
+        copy.start()
     for copy in own:
         copy.wait()
 
@@ -151,11 +160,15 @@
     def is_early(a):
         return pick(lambda m: time_start[a, m]) == 0
 
-    early = [None] + [is_early(a) for a in (1, 2)]
+    early = [is_early(a) for a in range(4)]
+
+    def soon_of(a):
+        return jnp.where(a < 2, jnp.where(a == 0, early[0], early[1]), jnp.where(a == 2, early[2], early[3]))
+
     low_lane = lax.broadcasted_iota(jnp.int32, (1, HD), 1) < HALF
 
-    def stat_row(buf, a, k):
-        rows = [buf[4 * a + i] for i in range(4)]
+    def stat_row(n, a, k):
+        rows = [stat_buf[4 * a + i, n] for i in range(4)]
         flipped = [pltpu.roll(row, HALF, 1) for row in rows]
         low = spot[k] == 0
         pairs = [
@@ -199,34 +212,46 @@
         later = window[k, pl.ds(4 * j + 4, 4)]
         return jnp.where(soon, now, later).reshape(4 * SPAN, HD)
 
-    def tokens(buf, k, a):
-        return buf[k, pl.ds(4 * a, 4)].reshape(4 * HALF, HD)
+    def tokens(n, k, a):
+        return qg_buf[k, pl.ds(4 * a, 4), n].reshape(4 * HALF, HD)
+
+    def send_queries(k):
+        @pl.loop(1, NT)
+        def _(d):
+            query_copy(k, peer(d)).start()
+
+        query_own(k).start()
 
     def probabilities(k):
         @pl.loop(1, NT)
         def _(d):
-            qg_copy(0, k, d).wait_recv()
+            qg_copy(k, d).wait_recv()
+
+        if k == 1:
+            send_queries(0)
 
         @pl.loop(0, 4)
         def _(a):
-            soon = is_early(a)
-            query = tokens(query_buf, k, a)
-            lse_row = stat_row(lse_buf, a, k) * LOG2E
+            soon = soon_of(a)
+            query = tokens(0, k, a)
+            lse_row = stat_row(0, a, k) * LOG2E
+            grad = tokens(1, k, a)
             for j in range(3):
                 scores = dot(tile(key_window, k, soon, j), query, ((1,), (1,)))
-                probs_buf[a, j] = jnp.exp2(scores * (SCALE * LOG2E) - lse_row)
-
-    def gradients(k):
-        @pl.loop(1, NT)
-        def _(d):
-            qg_copy(1, k, d).wait_recv()
-
-        @pl.loop(0, 4)
-        def _(a):
-            soon = is_early(a)
-            query = tokens(query_buf, k, a)
-            grad = tokens(grad_buf, k, a)
-            delta_row = stat_row(delta_buf, a, k)
+                probs = jnp.exp2(scores * (SCALE * LOG2E) - lse_row)
+                probs_buf[a, j] = probs
+                value_parts[k, 3 * a + j] = dot(
+                    probs.astype(jnp.bfloat16), grad, ((1,), (0,))
+                ).reshape(4, SPAN, HD)
+
+    def gradients(k, first, last):
+        @pl.loop(first, last)
+        def _(step):
+            a = lax.rem(step + ta // 4, 4)
+            soon = soon_of(a)
+            query = tokens(0, k, a)
+            grad = tokens(1, k, a)
+            delta_row = stat_row(1, a, k)
             turned = jnp.zeros((HD, 4 * HALF), jnp.float32)
             for j in range(3):
                 key = tile(key_window, k, soon, j)
@@ -234,24 +259,22 @@
                 probs = probs_buf[a, j]
                 dprob = dot(value, grad, ((1,), (1,)))
                 dscore = (probs * (dprob - delta_row)).astype(jnp.bfloat16)
-                value_parts[k, 3 * a + j] = dot(
-                    probs.astype(jnp.bfloat16), grad, ((1,), (0,))
-                ).reshape(4, SPAN, HD)
                 key_parts[k, 3 * a + j] = dot(dscore, query, ((1,), (0,))).reshape(4, SPAN, HD)
                 turned = turned + dot(key, dscore, ((0,), (0,)))
             query_low[k, pl.ds(4 * a, 4)] = (
                 (turned.T * SCALE).astype(jnp.bfloat16).reshape(4, HALF, HD)
             )
-            for i in range(4):
-                frame = 4 * a + i
-
-                @pl.when(frame != ta)
-                def _(frame=frame):
-                    query_copy(k, frame).start()
-
-                @pl.when(frame == ta)
-                def _():
-                    query_own(k).start()
+            if k == 1:
+                for i in range(4):
+                    frame = 4 * a + lax.rem(ta + i, 4)
+
+                    @pl.when(frame != ta)
+                    def _(frame=frame):
+                        query_copy(k, frame).start()
+
+                    @pl.when(frame == ta)
+                    def _():
+                        query_own(k).start()
 
     def over_time(parts, k):
         @pl.loop(0, 4)
@@ -301,75 +324,93 @@
         copy.start()
         back[n, k, s] = copy
 
-    for n in range(2):
-        @pl.loop(1, NT)
-        def _(d, n=n):
-            stat_copy(n, d).wait_recv()
+    def grad_ends(part):
+        low, out = ((pair_low.at[0], pair_out.at[:, rows_of(0), columns(head)]),
+                    (inner_low.at[1], pair_out.at[1, rows_of(1), columns(head)]),
+                    (inner_low.at[0], pair_out.at[0, rows_of(1), columns(head)]))[part]
+        return low, out
+
+    def grad_copy(part, d):
+        p = peer(d)
+        low, out = grad_ends(part)
+        return remote(low.at[p], out, kvo_ss.at[part, d], kvo_rs.at[part, d], (p, ha))
+
+    own_out = []
+
+    def add_up(n, k, low):
+        parts, recv, factor = ((key_parts, key_recv, SCALE), (value_parts, value_recv, 1.0))[n]
+        for s in range(2):
+            back[n, k, s].wait_recv()
+
+        @pl.loop(0, NT)
+        def _(frame):
+            whole = (
+                around(parts, frame, 2 + k)
+                + recv[0, k, frame].astype(jnp.float32)
+                + recv[1, k, frame].astype(jnp.float32)
+            )
+            low(frame)[...] = (whole * factor).astype(jnp.bfloat16)
+
+    def leave(part):
+        @pl.loop(1, NT)
+        def _(d):
+            grad_copy(part, d).start()
+
+        low, out = grad_ends(part)
+        copy = pltpu.make_async_copy(low.at[ta], out, own_sem.at[part])
+        copy.start()
+        own_out.append(copy)
+
+    def finish_inner(n):
+        add_up(n, 1, lambda frame: inner_low.at[n, frame])
+        leave(2 - n)
+
+    def finish_outer():
+        for n in (1, 0):
+            add_up(n, 0, lambda frame, n=n: pair_low.at[0, frame, n])
+        leave(0)
+
+    @pl.loop(1, NT)
+    def _(d):
+        stat_copy(d).wait_recv()
 
     for s in range(2):
         halos[s].wait_recv()
     choose_height(key_buf, key_window)
     probabilities(0)
+    over_time(value_parts, 0)
+    send_back(1, 0)
     for s in range(2):
         halos[2 + s].wait_recv()
     choose_height(value_buf, value_window)
-    gradients(0)
-    for n in (1, 0):
-        over_time((key_parts, value_parts)[n], 0)
-        send_back(n, 0)
+    gradients(0, 0, 4)
+    over_time(key_parts, 0)
+    send_back(0, 0)
     probabilities(1)
-    gradients(1)
-    for n in (1, 0):
-        over_time((key_parts, value_parts)[n], 1)
-        send_back(n, 4)
-    for e in (1, 5):
-        for n in (1, 0):
-            send_back(n, e)
-
-    def grad_copy(n, k, d):
-        p = peer(d)
-        low, out = ((key_low, key_out), (value_low, value_out))[n]
-        return remote(
-            low.at[k, p], out.at[rows_of(k), columns(head)],
-            kvo_ss.at[n, k, d], kvo_rs.at[n, k, d], (p, ha),
-        )
-
-    own_out = []
-    for k in (1, 0):
-        for n in (1, 0):
-            parts, recv, low, out = (
-                (key_parts, key_recv, key_low, key_out), (value_parts, value_recv, value_low, value_out)
-            )[n]
-            factor = SCALE if n == 0 else 1.0
-            for s in range(2):
-                back[n, k, s].wait_recv()
-
-            @pl.loop(0, NT)
-            def _(frame, parts=parts, recv=recv, low=low, factor=factor, k=k):
-                whole = (
-                    around(parts, frame, 2 + k)
-                    + recv[0, k, frame].astype(jnp.float32)
-                    + recv[1, k, frame].astype(jnp.float32)
-                )
-                low[k, frame] = (whole * factor).astype(jnp.bfloat16)
-
-            @pl.loop(1, NT)
-            def _(d, n=n, k=k):
-                grad_copy(n, k, d).start()
-
-            copy = pltpu.make_async_copy(
-                low.at[k, ta], out.at[rows_of(k), columns(head)], own_sem.at[2 * n + k]
-            )
-            copy.start()
-            own_out.append(copy)
+    over_time(value_parts, 1)
+    send_back(1, 1)
+    send_back(1, 4)
+    gradients(1, 0, 2)
+    finish_inner(1)
+    gradients(1, 2, 4)
+    over_time(key_parts, 1)
+    send_back(0, 1)
+    send_back(0, 4)
+    send_back(1, 5)
+    send_back(0, 5)
+    finish_inner(0)
+    finish_outer()
 
     for n in range(2):
         @pl.loop(1, NT)
         def _(d, n=n):
-            stat_copy(n, d).wait_send()
+            qg_copy(n, d).wait_send()
             kv_copy(n, d).wait_send()
-            for k in range(2):
-                qg_copy(n, k, d).wait_send()
+
+    @pl.loop(1, NT)
+    def _(d):
+        stat_copy(d).wait_send()
+
     for copy in halos + list(back.values()):
         copy.wait_send()
     for k in range(2):
@@ -385,18 +426,18 @@
             done.wait_send()
             done.wait_recv()
 
-    for n in range(2):
-        for k in range(2):
-            @pl.loop(1, NT)
-            def _(d, n=n, k=k):
-                grad_copy(n, k, d).wait()
+    for part in (1, 2, 0):
+        @pl.loop(1, NT)
+        def _(d, part=part):
+            grad_copy(part, d).wait()
 
     for copy in own_out:
         copy.wait()
 
 
-def move_kernel(*refs):
-    sources, targets, buf, in_sem, out_sem = refs[:3], refs[3:6], refs[6], refs[7], refs[8]
+def move_kernel(query, pair, *refs):
+    targets, buf, in_sem, out_sem = refs[:3], refs[3], refs[4], refs[5]
+    sources = (query, pair.at[0], pair.at[1])
     rows = [pl.ds(c * HALF, HALF) for c in range(2)]
     arrive = [
         pltpu.make_async_copy(sources[i].at[rows[c]], buf.at[i, rows[c]], in_sem.at[i, c])
@@ -427,36 +468,36 @@
     outs = pl.pallas_call(
         grads_kernel,
         name="tile_attention_grads",
-        out_shape=[jax.ShapeDtypeStruct((TOK, width), bf16)] * 3,
+        out_shape=[jax.ShapeDtypeStruct((TOK, width), bf16), jax.ShapeDtypeStruct((2, TOK, width), bf16)],
         in_specs=[smem] * 3 + [hbm] * 6,
-        out_specs=[hbm] * 3,
+        out_specs=[hbm] * 2,
         scratch_shapes=[
+            pltpu.VMEM((2, 2, HALF, width), bf16),
+            pltpu.VMEM((NT, 2, 1, TOK), f32),
             pltpu.VMEM((NT, 3 * TOK, HD), bf16),
             pltpu.VMEM((NT, 3 * TOK, HD), bf16),
-            pltpu.VMEM((2, NT, HALF, HD), bf16),
-            pltpu.VMEM((2, NT, HALF, HD), bf16),
-            pltpu.VMEM((NT, 1, TOK), f32),
-            pltpu.VMEM((NT, 1, TOK), f32),
+            pltpu.VMEM((2, NT, 2, HALF, HD), bf16),
+            pltpu.VMEM((NT, 2, 1, TOK), f32),
             pltpu.VMEM((2, NT, SPAN, HD), bf16),
             pltpu.VMEM((2, NT, SPAN, HD), bf16),
             pltpu.VMEM((4, 3, 4 * SPAN, 4 * HALF), f32),
             pltpu.VMEM((2, 12, 4, SPAN, HD), f32),
             pltpu.VMEM((2, 12, 4, SPAN, HD), f32),
             pltpu.VMEM((2, NT, HALF, HD), bf16),
-            pltpu.VMEM((2, NT, HALF, HD), bf16),
+            pltpu.VMEM((1, NT, 2, HALF, HD), bf16),
             pltpu.VMEM((2, NT, HALF, HD), bf16),
             pltpu.VMEM((2, 2, NT, HALF, HD), bf16),
             pltpu.VMEM((2, 2, NT, HALF, HD), bf16),
             pltpu.VMEM((2, 2, NT, HALF, HD), bf16),
             pltpu.VMEM((2, 2, NT, HALF, HD), bf16),
+            dma((NT,)), dma((NT,)),
             dma((2, NT)), dma((2, NT)),
             dma((2, NT)), dma((2, NT)),
-            dma((2, 2, NT)), dma((2, 2, NT)),
             dma((8,)),
             dma((2, 2)), dma((2, 2)),
             dma((2, 2, 2)), dma((2, 2, 2)),
             dma((2, NT)), dma((2, NT)),
-            dma((2, 2, NT)), dma((2, 2, NT)),
+            dma((3, NT)), dma((3, NT)),
         ],
         compiler_params=pltpu.CompilerParams(
             collective_id=0, has_side_effects=True, vmem_limit_bytes=60 * 2**20
@@ -466,7 +507,7 @@
         move_kernel,
         name="place_grads",
         out_shape=[jax.ShapeDtypeStruct((TOK, width), bf16)] * 3,
-        in_specs=[hbm] * 3,
+        in_specs=[hbm] * 2,
         out_specs=[hbm] * 3,
         scratch_shapes=[pltpu.VMEM((3, TOK, width), bf16), dma((3, 2)), dma((3, 2))],
         compiler_params=pltpu.CompilerParams(vmem_limit_bytes=60 * 2**20),

time: 107 us -> 105 us (0.981)
  Pallas kernels: 106 us -> 104 us
    pallas_call x1, Pallas kernels: 103 us -> 101 us  [per_device(): pl.pallas_call(grads_kernel, name='tile_attention_grads', out_shape=[jax....]
where the time goes in v4:
time: 105 us; the launch traced here: 104 us
  Pallas kernels  104 us (99%)
    pallas_call x1, Pallas kernels, per_device(): pl.pallas_call(grads_kernel, name='tile_attention_grads', out_shape=[jax....  101 us
    pallas_call x1, Pallas kernels, per_device(): pl.pallas_call(move_kernel, name='place_grads', out_shape=[jax.ShapeDtype...  2.19 us

profile of v4, /device:TPU:1, one launch (start us, length us, event | category | flops | bytes accessed | tf_op | source)
XLA Modules:
  0.0 104.3 jit_solution(15824159838502884872)
XLA Ops:
  0.6 101.5 %tile_attention_grads.1 = (bf16[128,2048]{1,0:T(8,128)(2,1)}, bf16[2,128,2048]{2,1,0:T(8,128)(2,1)}) custom-call(s32[16]{0:T(128)} %order.1, s32[4,16]{1,0:T(4,128)} %bitcast.12, s32[16,64]{1,0:T(8,128)} %height_start.1, f32[16,1,128]{2,1,0:T(1,128)} %lse.1, f32[16,1,128]{2,1,0:T(1,128)} %delta.1, bf16[128,2048]{1,0:T(8,128)(2,1)} %bitcast.8, ...), custom_call_target="tpu_custom_call" | custom-call | tf_op jit(solution)/shard_map/tile_attention_grads/pallas_call | solution.py:468
  102.1 2.2 %place_grads.1 = (bf16[128,2048]{1,0:T(8,128)(2,1)}, bf16[128,2048]{1,0:T(8,128)(2,1)}, bf16[128,2048]{1,0:T(8,128)(2,1)}) custom-call(bf16[128,2048]{1,0:T(8,128)(2,1)} %get-tuple-element.8.query, bf16[2,128,2048]{2,1,0:T(8,128)(2,1)} %get-tuple-element.9.pair), custom_call_target="tpu_custom_call" | custom-call | tf_op jit(solution)/shard_map/place_grads/pallas_call | solution.py:506

commit v5 on v4

--- a/solution.py
+++ b/solution.py
@@ -65,33 +65,6 @@
 
     for side in sides:
         pl.semaphore_signal(barrier, inc=1, device_id=side, device_id_type=MESH)
-    pl.semaphore_wait(barrier, NT + 1)
-
-    def remote(src, dst, send_sem, recv_sem, device):
-        return pltpu.make_async_remote_copy(
-            src_ref=src, dst_ref=dst, send_sem=send_sem, recv_sem=recv_sem,
-            device_id=device, device_id_type=MESH,
-        )
-
-    def stat_copy(d):
-        p = peer(d)
-        return remote(stat_stage.at[head_of(p)], stat_buf.at[ta], stat_ss.at[d], stat_rs.at[d], (p, ha))
-
-    def kv_copy(n, d):
-        p = peer(d)
-        src, dst = ((keys, key_buf), (values, value_buf))[n]
-        return remote(
-            src.at[:, columns(head_of(p))], dst.at[ta, pl.ds(TOK, TOK), :],
-            kv_ss.at[n, d], kv_rs.at[n, d], (p, ha),
-        )
-
-    def qg_copy(k, d):
-        p = peer(d)
-        return remote(
-            qg_stage.at[k, :, :, columns(head_of(p))], qg_buf.at[k, ta],
-            qg_ss.at[k, d], qg_rs.at[k, d], (p, ha),
-        )
-
     staged = [
         pltpu.make_async_copy(src, stat_stage.at[:, n], own_sem.at[n]) for n, src in enumerate((lse, delta))
     ]
@@ -100,6 +73,33 @@
             staged.append(pltpu.make_async_copy(src.at[rows_of(k), :], qg_stage.at[k, n], own_sem.at[2 + 2 * k + n]))
     for copy in staged:
         copy.start()
+
+    pl.semaphore_wait(barrier, NT + 1)
+
+    def remote(src, dst, send_sem, recv_sem, device):
+        return pltpu.make_async_remote_copy(
+            src_ref=src, dst_ref=dst, send_sem=send_sem, recv_sem=recv_sem,
+            device_id=device, device_id_type=MESH,
+        )
+
+    def stat_copy(d):
+        p = peer(d)
+        return remote(stat_stage.at[head_of(p)], stat_buf.at[ta], stat_ss.at[d], stat_rs.at[d], (p, ha))
+
+    def kv_copy(n, d):
+        p = peer(d)
+        src, dst = ((keys, key_buf), (values, value_buf))[n]
+        return remote(
+            src.at[:, columns(head_of(p))], dst.at[ta, pl.ds(TOK, TOK), :],
+            kv_ss.at[n, d], kv_rs.at[n, d], (p, ha),
+        )
+
+    def qg_copy(k, d):
+        p = peer(d)
+        return remote(
+            qg_stage.at[k, :, :, columns(head_of(p))], qg_buf.at[k, ta],
+            qg_ss.at[k, d], qg_rs.at[k, d], (p, ha),
+        )
 
     for n in range(2):
         @pl.loop(1, NT)
@@ -230,7 +230,7 @@
         if k == 1:
             send_queries(0)
 
-        @pl.loop(0, 4)
+        @pl.loop(0, 4, unroll=2)
         def _(a):
             soon = soon_of(a)
             query = tokens(0, k, a)
@@ -245,7 +245,7 @@
                 ).reshape(4, SPAN, HD)
 
     def gradients(k, first, last):
-        @pl.loop(first, last)
+        @pl.loop(first, last, unroll=2)
         def _(step):
             a = lax.rem(step + ta // 4, 4)
             soon = soon_of(a)
@@ -277,7 +277,7 @@
                         query_own(k).start()
 
     def over_time(parts, k):
-        @pl.loop(0, 4)
+        @pl.loop(0, 4, unroll=2)
         def _(i):
             def entry(a, j):
                 return parts[k, 3 * a + j, i]
@@ -314,7 +314,7 @@
         parts, send, recv = ((key_parts, key_send, key_recv), (value_parts, value_send, value_recv))[n]
         s, k = e // 4, (e + 1) % 2
 
-        @pl.loop(0, NT)
+        @pl.loop(0, NT, unroll=4)
         def _(frame):
             send[s, k, frame] = around(parts, frame, e).astype(jnp.bfloat16)
 
@@ -342,7 +342,7 @@
         for s in range(2):
             back[n, k, s].wait_recv()
 
-        @pl.loop(0, NT)
+        @pl.loop(0, NT, unroll=4)
         def _(frame):
             whole = (
                 around(parts, frame, 2 + k)
@@ -396,9 +396,9 @@
     over_time(key_parts, 1)
     send_back(0, 1)
     send_back(0, 4)
+    finish_inner(0)
     send_back(1, 5)
     send_back(0, 5)
-    finish_inner(0)
     finish_outer()
 
     for n in range(2):

time: 105 us -> 103 us (0.981)
  Pallas kernels: 104 us -> 102 us
    pallas_call x1, Pallas kernels: 101 us -> 99.9 us  [per_device(): pl.pallas_call(grads_kernel, name='tile_attention_grads', out_shape=[jax....]
where the time goes in v5:
time: 103 us
  Pallas kernels  102 us (99%)
    pallas_call x1, Pallas kernels, per_device(): pl.pallas_call(grads_kernel, name='tile_attention_grads', out_shape=[jax....  99.9 us
    pallas_call x1, Pallas kernels, per_device(): pl.pallas_call(move_kernel, name='place_grads', out_shape=[jax.ShapeDtype...  2.19 us

profile of v5, /device:TPU:1, one launch (start us, length us, event | category | flops | bytes accessed | tf_op | source)
XLA Modules:
  0.0 102.7 jit_solution(10116331031424974420)
XLA Ops:
  0.6 99.9 %tile_attention_grads.1 = (bf16[128,2048]{1,0:T(8,128)(2,1)}, bf16[2,128,2048]{2,1,0:T(8,128)(2,1)}) custom-call(s32[16]{0:T(128)} %order.1, s32[4,16]{1,0:T(4,128)} %bitcast.12, s32[16,64]{1,0:T(8,128)} %height_start.1, f32[16,1,128]{2,1,0:T(1,128)} %lse.1, f32[16,1,128]{2,1,0:T(1,128)} %delta.1, bf16[128,2048]{1,0:T(8,128)(2,1)} %bitcast.8, ...), custom_call_target="tpu_custom_call" | custom-call | tf_op jit(solution)/shard_map/tile_attention_grads/pallas_call | solution.py:468
  100.5 2.2 %place_grads.1 = (bf16[128,2048]{1,0:T(8,128)(2,1)}, bf16[128,2048]{1,0:T(8,128)(2,1)}, bf16[128,2048]{1,0:T(8,128)(2,1)}) custom-call(bf16[128,2048]{1,0:T(8,128)(2,1)} %get-tuple-element.8.query, bf16[2,128,2048]{2,1,0:T(8,128)(2,1)} %get-tuple-element.9.pair), custom_call_target="tpu_custom_call" | custom-call | tf_op jit(solution)/shard_map/place_grads/pallas_call | solution.py:506

commit v6 on v5

--- a/solution.py
+++ b/solution.py
@@ -388,14 +388,14 @@
     send_back(0, 0)
     probabilities(1)
     over_time(value_parts, 1)
+    send_back(1, 4)
     send_back(1, 1)
-    send_back(1, 4)
     gradients(1, 0, 2)
     finish_inner(1)
     gradients(1, 2, 4)
     over_time(key_parts, 1)
+    send_back(0, 4)
     send_back(0, 1)
-    send_back(0, 4)
     finish_inner(0)
     send_back(1, 5)
     send_back(0, 5)

time: 103 us -> 103 us (level)
  no operation moved by 1% of the time
where the time goes in v6:
time: 103 us
  Pallas kernels  102 us (99%)
    pallas_call x1, Pallas kernels, per_device(): pl.pallas_call(grads_kernel, name='tile_attention_grads', out_shape=[jax....  99.8 us
    pallas_call x1, Pallas kernels, per_device(): pl.pallas_call(move_kernel, name='place_grads', out_shape=[jax.ShapeDtype...  2.19 us

profile of v6, /device:TPU:1, one launch (start us, length us, event | category | flops | bytes accessed | tf_op | source)
XLA Modules:
  0.0 102.6 jit_solution(6903153417209407203)
XLA Ops:
  0.6 99.8 %tile_attention_grads.1 = (bf16[128,2048]{1,0:T(8,128)(2,1)}, bf16[2,128,2048]{2,1,0:T(8,128)(2,1)}) custom-call(s32[16]{0:T(128)} %order.1, s32[4,16]{1,0:T(4,128)} %bitcast.12, s32[16,64]{1,0:T(8,128)} %height_start.1, f32[16,1,128]{2,1,0:T(1,128)} %lse.1, f32[16,1,128]{2,1,0:T(1,128)} %delta.1, bf16[128,2048]{1,0:T(8,128)(2,1)} %bitcast.8, ...), custom_call_target="tpu_custom_call" | custom-call | tf_op jit(solution)/shard_map/tile_attention_grads/pallas_call | solution.py:468
  100.4 2.2 %place_grads.1 = (bf16[128,2048]{1,0:T(8,128)(2,1)}, bf16[128,2048]{1,0:T(8,128)(2,1)}, bf16[128,2048]{1,0:T(8,128)(2,1)}) custom-call(bf16[128,2048]{1,0:T(8,128)(2,1)} %get-tuple-element.8.query, bf16[2,128,2048]{2,1,0:T(8,128)(2,1)} %get-tuple-element.9.pair), custom_call_target="tpu_custom_call" | custom-call | tf_op jit(solution)/shard_map/place_grads/pallas_call | solution.py:506
